TPU v7x, 256 devices: a whole 4x4x8 slice. The times are simulated.
256 devices in a mesh: grp: 32 (over y, z), sp: 8 (over x, core).
Axes of the slice: x: 4, y: 4, z: 8, core: 2. Of those that a mesh axis runs over, the one named last changes fastest.
Arguments:
- queries: bfloat16 [32768, 4096], P(('grp', 'sp')), may hold values from -5 to 5
- key_row_matrix: bfloat16 [32768, 1024], P(('grp', 'sp')), may hold values from -5 to 5
- value_row_matrix: bfloat16 [32768, 1024], P(('grp', 'sp')), may hold values from -6 to 6
- out_grad: bfloat16 [32768, 4096], P(('grp', 'sp')), may hold values from -6 to 6
- dest_group: int32 [32, 1024], P('grp', 'sp'), may hold values from 0 to 31, as said below
- source_group: int32 [32, 1024], P('grp', 'sp'), may hold values from 0 to 31, as said below
- seq_start: int32 [32, 1024], P('grp'), may hold values from 0 to 768, as said below
Outputs:
- attended: bfloat16 [32768, 4096], P(('grp', 'sp'))
- query_grad: bfloat16 [32768, 4096], P(('grp', 'sp'))
- key_gradient: bfloat16 [32768, 1024], P(('grp', 'sp'))
- value_gradient: bfloat16 [32768, 1024], P(('grp', 'sp'))
Inputs may be any that keep to these rules, and one draw needn't show every extreme that they name: `dest_group`: for each index s of sp and groups g, g2, the tokens of device (g, s) sent to g2 are as many as the positions of column s of group g2 whose source is g; this count is even, at most 8, and equals 8 for some pair in every column. Entries come in equal aligned pairs (i even, i + 1). `source_group`: the counterpart of dest_group: entries come in equal aligned pairs, and each group source count matches dest_group as stated there. `seq_start`: Even, at most the position itself, equal for all positions of one sequence and rising only where a sequence begins; a group holds one or two sequences.
All inputs are finite; a program needn't handle non-finite values.
Results may differ from a plain program's by a relative error of at most 0.0072.
Values may be sent and summed in bfloat16 or wider, within the bound.
No kernel may reach another device: no remote copies, remote signals or barrier semaphores. Data moves between devices by JAX's collectives and lax.ppermute only.
A program may use at most 128 MiB of HBM per device.

v0:
```python
import math

import jax
import jax.numpy as jnp
from jax import lax
from jax.sharding import PartitionSpec as P

HEAD_SIZE = 128


def rank_within(labels, count):
    marks = (labels[:, None] == jnp.arange(count, dtype=jnp.int32)[None, :]).astype(jnp.int32)
    before = jnp.cumsum(marks, axis=0) - marks
    return jnp.sum(before * marks, axis=1)


def head_block(query_part, grad_part, positions, starts, key_part, value_part, scaling):
    key_place = jnp.arange(key_part.shape[0], dtype=jnp.int32)
    visible = (key_place[None, :] >= starts[:, None]) & (key_place[None, :] <= positions[:, None])
    across = (((1,), (1,)), ((), ()))
    downward = (((0,), (0,)), ((), ()))
    scores = (
        lax.dot_general(query_part, key_part, across, preferred_element_type=jnp.float32) * scaling
    )
    scores = jnp.where(visible, scores, -jnp.inf)
    powers = jnp.exp(scores - jnp.max(scores, axis=1, keepdims=True))
    probability = powers / jnp.sum(powers, axis=1, keepdims=True)
    weights = probability.astype(jnp.bfloat16)
    output = jnp.dot(weights, value_part, preferred_element_type=jnp.float32).astype(jnp.bfloat16)
    prob_grad = lax.dot_general(grad_part, value_part, across, preferred_element_type=jnp.float32)
    spread = jnp.sum(probability * prob_grad, axis=1, keepdims=True)
    dscore = (probability * (prob_grad - spread) * scaling).astype(jnp.bfloat16)
    grad_query = jnp.dot(dscore, key_part, preferred_element_type=jnp.float32).astype(jnp.bfloat16)
    key_gradient_fn = lax.dot_general(
        dscore, query_part, downward, preferred_element_type=jnp.float32
    )
    value_gradient_fn = lax.dot_general(
        weights, grad_part, downward, preferred_element_type=jnp.float32
    )
    return (output, grad_query, key_gradient_fn, value_gradient_fn)


def attend_causal(query_rows, key_all, value_all, grad_rows, starts):
    query_count = query_rows.shape[0]
    key_count = key_all.shape[0]
    group_share = query_rows.shape[1] // key_all.shape[1]
    flat_rows = query_count * group_share
    block_rows = 512
    scaling = 1.0 / math.sqrt(HEAD_SIZE)
    head_width = group_share * HEAD_SIZE
    positions = jnp.arange(query_count, dtype=jnp.int32)
    pos_rows = jnp.broadcast_to(positions[:, None], (query_count, group_share)).reshape(flat_rows)
    start_rows = jnp.broadcast_to(starts[:, None], (query_count, group_share)).reshape(flat_rows)
    outputs, query_grads, key_grads, value_grads = ([], [], [], [])
    query_head = query_rows.reshape(flat_rows, HEAD_SIZE)
    grad_head = grad_rows.reshape(flat_rows, HEAD_SIZE)
    block_outs = []
    block_grads = []
    key_total = jnp.zeros((key_count, HEAD_SIZE), jnp.float32)
    value_total = jnp.zeros((key_count, HEAD_SIZE), jnp.float32)
    for block_index in range(flat_rows // block_rows):
        first = block_index * block_rows
        key_end = min(key_count, (first + block_rows) // group_share)
        result = head_block(
            query_head[first : first + block_rows],
            grad_head[first : first + block_rows],
            pos_rows[first : first + block_rows],
            start_rows[first : first + block_rows],
            key_all[:key_end],
            value_all[:key_end],
            scaling,
        )
        block_outs.append(result[0])
        block_grads.append(result[1])
        key_total = key_total + jnp.pad(result[2], ((0, key_count - key_end), (0, 0)))
        value_total = value_total + jnp.pad(result[3], ((0, key_count - key_end), (0, 0)))
    outputs.append(jnp.concatenate(block_outs, axis=0).reshape(query_count, head_width))
    query_grads.append(jnp.concatenate(block_grads, axis=0).reshape(query_count, head_width))
    key_grads.append(key_total)
    value_grads.append(value_total)
    return (outputs[0], query_grads[0], key_grads[0], value_grads[0])


def pack_rows(source_rows, slots, total):
    return jnp.zeros((total, source_rows.shape[1]), source_rows.dtype).at[slots].set(source_rows)


def per_device(
    queries, key_row_matrix, value_row_matrix, out_grad, dest_group, source_group, seq_start
):
    groups = lax.axis_size("grp")
    tok_rows = queries.shape[0]
    capacity = 2 * tok_rows // groups
    total = groups * capacity
    destination = dest_group.reshape(tok_rows)
    anchor = source_group.reshape(tok_rows)
    send_slot = destination * capacity + rank_within(destination, groups)
    recv_slot = anchor * capacity + rank_within(anchor, groups)
    arrived = (
        lax.all_to_all(
            pack_rows(queries, send_slot, total), "grp", split_axis=0, concat_axis=0, tiled=True
        ),
        lax.all_to_all(
            pack_rows(key_row_matrix, send_slot, total),
            "grp",
            split_axis=0,
            concat_axis=0,
            tiled=True,
        ),
        lax.all_to_all(
            pack_rows(value_row_matrix, send_slot, total),
            "grp",
            split_axis=0,
            concat_axis=0,
            tiled=True,
        ),
        lax.all_to_all(
            pack_rows(out_grad, send_slot, total), "grp", split_axis=0, concat_axis=0, tiled=True
        ),
    )
    query_seq = arrived[0][recv_slot]
    key_seq = arrived[1][recv_slot]
    value_seq = arrived[2][recv_slot]
    grad_seq = arrived[3][recv_slot]
    starts = seq_start.reshape(-1)
    query_head, key_head, value_head, grad_head = (
        lax.all_to_all(query_seq, "sp", split_axis=1, concat_axis=0, tiled=True),
        lax.all_to_all(key_seq, "sp", split_axis=1, concat_axis=0, tiled=True),
        lax.all_to_all(value_seq, "sp", split_axis=1, concat_axis=0, tiled=True),
        lax.all_to_all(grad_seq, "sp", split_axis=1, concat_axis=0, tiled=True),
    )
    output, grad_query, key_gradient_fn, value_gradient_fn = attend_causal(
        query_head, key_head, value_head, grad_head, starts
    )
    output, grad_query, key_gradient_fn, value_gradient_fn = (
        lax.all_to_all(output, "sp", split_axis=0, concat_axis=1, tiled=True),
        lax.all_to_all(grad_query, "sp", split_axis=0, concat_axis=1, tiled=True),
        lax.all_to_all(
            key_gradient_fn.astype(jnp.bfloat16), "sp", split_axis=0, concat_axis=1, tiled=True
        ),
        lax.all_to_all(
            value_gradient_fn.astype(jnp.bfloat16), "sp", split_axis=0, concat_axis=1, tiled=True
        ),
    )
    returned = (
        lax.all_to_all(
            pack_rows(output, recv_slot, total), "grp", split_axis=0, concat_axis=0, tiled=True
        ),
        lax.all_to_all(
            pack_rows(grad_query, recv_slot, total), "grp", split_axis=0, concat_axis=0, tiled=True
        ),
        lax.all_to_all(
            pack_rows(key_gradient_fn, recv_slot, total),
            "grp",
            split_axis=0,
            concat_axis=0,
            tiled=True,
        ),
        lax.all_to_all(
            pack_rows(value_gradient_fn, recv_slot, total),
            "grp",
            split_axis=0,
            concat_axis=0,
            tiled=True,
        ),
    )
    return (
        returned[0][send_slot],
        returned[1][send_slot],
        returned[2][send_slot],
        returned[3][send_slot],
    )


def solution(mesh):
    in_specs = (
        P(("grp", "sp"), None),
        P(("grp", "sp"), None),
        P(("grp", "sp"), None),
        P(("grp", "sp"), None),
        P("grp", "sp"),
        P("grp", "sp"),
        P("grp", None),
    )
    out_specs = (
        P(("grp", "sp"), None),
        P(("grp", "sp"), None),
        P(("grp", "sp"), None),
        P(("grp", "sp"), None),
    )
    return jax.shard_map(
        per_device, mesh=mesh, in_specs=in_specs, out_specs=out_specs, check_vma=False
    )
```

profile of v0, /device:TPU:32, one launch (start us, length us, event | category | flops | bytes accessed | tf_op | source)
XLA Modules:
  0.0 511.8 jit_solution(13076751112003703941)
XLA Ops:
  5.4 11.4 %all-to-all-start.4 = ((bf16[32,8,1024]{2,1,0:T(8,128)(2,1)}), bf16[32,8,1024]{2,1,0:T(8,128)(2,1)S(1)}, u32[]{:S(2)}, u32[]{:S(2)}) async-start(bf16[32,8,1024]{2,1,0:T(8,128)(2,1)} %bitcast.16), calls=%async_computation.4 | async-start | bytes 1048576 | tf_op jit(solution)/shard_map/all_to_all | solution.py:110
  19.2 15.2 %all-to-all-done.4 = bf16[32,8,1024]{2,1,0:T(8,128)(2,1)S(1)} async-done(((bf16[32,8,1024]{2,1,0:T(8,128)(2,1)}), bf16[32,8,1024]{2,1,0:T(8,128)(2,1)S(1)}, u32[]{:S(2)}, u32[]{:S(2)}) %all-to-all-start.4) | async-done | bytes 524320 | tf_op jit(solution)/shard_map/all_to_all | solution.py:110
  34.4 4.9 all-to-all-start.2
  41.9 14.4 %all-to-all-done.2 = bf16[32,8,1024]{2,1,0:T(8,128)(2,1)S(1)} async-done(((bf16[32,8,1024]{2,1,0:T(8,128)(2,1)}), bf16[32,8,1024]{2,1,0:T(8,128)(2,1)S(1)}, u32[]{:S(2)}, u32[]{:S(2)}) %all-to-all-start.2) | async-done | bytes 524320 | tf_op jit(solution)/shard_map/all_to_all | solution.py:103
  62.1 5.9 %all-to-all-done.5 = bf16[128,8,128]{2,0,1:T(8,128)(2,1)S(1)} async-done(((bf16[128,8,128]{2,0,1:T(8,128)(2,1)}), bf16[128,8,128]{2,0,1:T(8,128)(2,1)S(1)}, u32[]{:S(2)}, u32[]{:S(2)}) %all-to-all-start.5) | async-done | bytes 262176 | tf_op jit(solution)/shard_map/all_to_all | solution.py:129
  78.9 4.9 all-to-all-start.8
  88.2 44.7 %all-to-all-done.8 = bf16[32,8,4096]{2,1,0:T(8,128)(2,1)S(1)} async-done(((bf16[32,8,4096]{2,1,0:T(8,128)(2,1)}), bf16[32,8,4096]{2,1,0:T(8,128)(2,1)S(1)}, u32[]{:S(2)}, u32[]{:S(2)}) %all-to-all-start.8) | async-done | bytes 2097184 | tf_op jit(solution)/shard_map/all_to_all | solution.py:117
  134.2 7.1 %all-to-all-start = ((bf16[32,8,4096]{2,1,0:T(8,128)(2,1)}), bf16[32,8,4096]{2,1,0:T(8,128)(2,1)S(1)}, u32[]{:S(2)}, u32[]{:S(2)}) async-start(bf16[32,8,4096]{2,1,0:T(8,128)(2,1)} %bitcast.207), calls=%async_computation | async-start | bytes 4194304 | tf_op jit(solution)/shard_map/all_to_all | solution.py:100
  141.3 5.0 gather_fusion.4
  148.7 41.9 %all-to-all-done = bf16[32,8,4096]{2,1,0:T(8,128)(2,1)S(1)} async-done(((bf16[32,8,4096]{2,1,0:T(8,128)(2,1)}), bf16[32,8,4096]{2,1,0:T(8,128)(2,1)S(1)}, u32[]{:S(2)}, u32[]{:S(2)}) %all-to-all-start) | async-done | bytes 2097184 | tf_op jit(solution)/shard_map/all_to_all | solution.py:100
  205.1 5.6 %all-to-all-done.9 = bf16[128,8,512]{2,0,1:T(8,128)(2,1)} async-done(((bf16[128,8,512]{2,0,1:T(8,128)(2,1)}), bf16[128,8,512]{2,0,1:T(8,128)(2,1)}, u32[]{:S(2)}, u32[]{:S(2)}) %all-to-all-start.9) | async-done | bytes 1048608 | tf_op jit(solution)/shard_map/all_to_all | solution.py:130
  225.2 5.0 all-to-all-done.1
  256.9 9.5 %fusion.114 = (f32[512]{0:T(512)S(1)}, f32[512,768]{1,0:T(8,128)S(1)}) fusion(bf16[512,128]{1,0:T(8,128)(2,1)S(1)} %slice.325, bf16[768,128]{1,0:T(8,128)(2,1)S(1)} %bitcast.239, s32[512]{0:T(512)S(1)} %le.119, s32[512]{0:T(512)S(1)} %ge.162), kind=kOutput, calls=%fused_computation.212 | convolution fusion | flops 103022080 | bytes 1906688 | tf_op jit(solution)/shard_map/dot_general | solution.py:23
  303.6 6.4 %all-to-all-done.12 = bf16[8,128,128]{1,2,0:T(8,128)(2,1)S(1)} async-done(((bf16[8,128,128]{1,2,0:T(8,128)(2,1)}), bf16[8,128,128]{1,2,0:T(8,128)(2,1)S(1)}, u32[]{:S(2)}, u32[]{:S(2)}) %all-to-all-start.12) | async-done | bytes 262176 | tf_op jit(solution)/shard_map/all_to_all | solution.py:138
  324.5 5.8 %all-to-all-done.6 = bf16[8,128,512]{1,2,0:T(8,128)(2,1)} async-done(((bf16[8,128,512]{1,2,0:T(8,128)(2,1)}), bf16[8,128,512]{1,2,0:T(8,128)(2,1)}, u32[]{:S(2)}, u32[]{:S(2)}) %all-to-all-start.6) | async-done | bytes 1048608 | tf_op jit(solution)/shard_map/all_to_all | solution.py:136
  337.0 12.7 %all-to-all-done.10 = bf16[8,128,512]{1,2,0:T(8,128)(2,1)S(1)} async-done(((bf16[8,128,512]{1,2,0:T(8,128)(2,1)}), bf16[8,128,512]{1,2,0:T(8,128)(2,1)S(1)}, u32[]{:S(2)}, u32[]{:S(2)}) %all-to-all-start.10) | async-done | bytes 1048608 | tf_op jit(solution)/shard_map/all_to_all | solution.py:137
  350.7 6.4 %all-to-all-start.15 = ((bf16[32,8,1024]{2,1,0:T(8,128)(2,1)}), bf16[32,8,1024]{2,1,0:T(8,128)(2,1)S(1)}, u32[]{:S(2)}, u32[]{:S(2)}) async-start(bf16[32,8,1024]{2,1,0:T(8,128)(2,1)} %bitcast.62), calls=%async_computation.15 | async-start | bytes 1048576 | tf_op jit(solution)/shard_map/all_to_all | solution.py:159
  359.3 15.2 %all-to-all-done.15 = bf16[32,8,1024]{2,1,0:T(8,128)(2,1)S(1)} async-done(((bf16[32,8,1024]{2,1,0:T(8,128)(2,1)}), bf16[32,8,1024]{2,1,0:T(8,128)(2,1)S(1)}, u32[]{:S(2)}, u32[]{:S(2)}) %all-to-all-start.15) | async-done | bytes 524320 | tf_op jit(solution)/shard_map/all_to_all | solution.py:159
  384.5 11.7 %all-to-all-done.13 = bf16[32,8,1024]{2,1,0:T(8,128)(2,1)S(1)} async-done(((bf16[32,8,1024]{2,1,0:T(8,128)(2,1)}), bf16[32,8,1024]{2,1,0:T(8,128)(2,1)S(1)}, u32[]{:S(2)}, u32[]{:S(2)}) %all-to-all-start.13) | async-done | bytes 524320 | tf_op jit(solution)/shard_map/all_to_all | solution.py:152
  396.3 4.9 all-to-all-start.7
  407.7 42.8 %all-to-all-done.7 = bf16[32,8,4096]{2,1,0:T(8,128)(2,1)S(1)} async-done(((bf16[32,8,4096]{2,1,0:T(8,128)(2,1)}), bf16[32,8,4096]{2,1,0:T(8,128)(2,1)S(1)}, u32[]{:S(2)}, u32[]{:S(2)}) %all-to-all-start.7) | async-done | bytes 2097184 | tf_op jit(solution)/shard_map/all_to_all | solution.py:146
  450.5 6.6 %all-to-all-start.11 = ((bf16[32,8,4096]{2,1,0:T(8,128)(2,1)}), bf16[32,8,4096]{2,1,0:T(8,128)(2,1)}, u32[]{:S(2)}, u32[]{:S(2)}) async-start(bf16[32,8,4096]{2,1,0:T(8,128)(2,1)} %bitcast.205), calls=%async_computation.11 | async-start | bytes 4194304 | tf_op jit(solution)/shard_map/all_to_all | solution.py:149
  462.4 43.9 %all-to-all-done.11 = bf16[32,8,4096]{2,1,0:T(8,128)(2,1)} async-done(((bf16[32,8,4096]{2,1,0:T(8,128)(2,1)}), bf16[32,8,4096]{2,1,0:T(8,128)(2,1)}, u32[]{:S(2)}, u32[]{:S(2)}) %all-to-all-start.11) | async-done | bytes 2097184 | tf_op jit(solution)/shard_map/all_to_all | solution.py:149
  506.4 5.0 gather_fusion.5
  (283 shorter events, 172.8 us)
Async XLA Ops:
  0.6 38.7 %copy-start.41 = (s32[1,128]{1,0:T(1,128)S(1)}, s32[1,128]{1,0:T(1,128)}, u32[]{:S(2)}) copy-start(s32[1,128]{1,0:T(1,128)} %param.12) | copy-start | bytes 1540
  3.1 80.8 %copy-start.50 = (s32[128]{0:T(128)}, s32[128]{0:T(128)S(1)}, u32[]{:S(2)}) copy-start(s32[128]{0:T(128)S(1)} %fusion.90) | copy-start | bytes 1540
  5.4 29.0 %all-to-all-start.4 = ((bf16[32,8,1024]{2,1,0:T(8,128)(2,1)}), bf16[32,8,1024]{2,1,0:T(8,128)(2,1)S(1)}, u32[]{:S(2)}, u32[]{:S(2)}) async-start(bf16[32,8,1024]{2,1,0:T(8,128)(2,1)} %bitcast.16), calls=%async_computation.4 | async-start | bytes 1048576 | tf_op jit(solution)/shard_map/all_to_all | solution.py:110
  34.4 21.8 %all-to-all-start.2 = ((bf16[32,8,1024]{2,1,0:T(8,128)(2,1)}), bf16[32,8,1024]{2,1,0:T(8,128)(2,1)S(1)}, u32[]{:S(2)}, u32[]{:S(2)}) async-start(bf16[32,8,1024]{2,1,0:T(8,128)(2,1)} %bitcast.12), calls=%async_computation.2 | async-start | bytes 1048576 | tf_op jit(solution)/shard_map/all_to_all | solution.py:103
  56.2 11.8 %all-to-all-start.5 = ((bf16[128,8,128]{2,0,1:T(8,128)(2,1)}), bf16[128,8,128]{2,0,1:T(8,128)(2,1)S(1)}, u32[]{:S(2)}, u32[]{:S(2)}) async-start(bf16[128,8,128]{2,0,1:T(8,128)(2,1)} %copy_bitcast_fusion.2), calls=%async_computation.5 | async-start | bytes 524288 | tf_op jit(solution)/shard_map/all_to_all | solution.py:129
  68.1 10.9 %all-to-all-start.3 = ((bf16[128,8,128]{2,0,1:T(8,128)(2,1)}), bf16[128,8,128]{2,0,1:T(8,128)(2,1)S(1)}, u32[]{:S(2)}, u32[]{:S(2)}) async-start(bf16[128,8,128]{2,0,1:T(8,128)(2,1)} %copy_bitcast_fusion.3), calls=%async_computation.3 | async-start | bytes 524288 | tf_op jit(solution)/shard_map/all_to_all | solution.py:128
  78.9 53.9 %all-to-all-start.8 = ((bf16[32,8,4096]{2,1,0:T(8,128)(2,1)}), bf16[32,8,4096]{2,1,0:T(8,128)(2,1)S(1)}, u32[]{:S(2)}, u32[]{:S(2)}) async-start(bf16[32,8,4096]{2,1,0:T(8,128)(2,1)} %bitcast.208), calls=%async_computation.8 | async-start | bytes 4194304 | tf_op jit(solution)/shard_map/all_to_all | solution.py:117
  134.2 56.4 %all-to-all-start = ((bf16[32,8,4096]{2,1,0:T(8,128)(2,1)}), bf16[32,8,4096]{2,1,0:T(8,128)(2,1)S(1)}, u32[]{:S(2)}, u32[]{:S(2)}) async-start(bf16[32,8,4096]{2,1,0:T(8,128)(2,1)} %bitcast.207), calls=%async_computation | async-start | bytes 4194304 | tf_op jit(solution)/shard_map/all_to_all | solution.py:100
  146.3 48.5 %copy-start.40 = (s32[1,1024]{1,0:T(1,128)S(1)}, s32[1,1024]{1,0:T(1,128)}, u32[]{:S(2)}) copy-start(s32[1,1024]{1,0:T(1,128)} %param.13) | copy-start | bytes 12292
  190.5 20.2 %all-to-all-start.9 = ((bf16[128,8,512]{2,0,1:T(8,128)(2,1)}), bf16[128,8,512]{2,0,1:T(8,128)(2,1)}, u32[]{:S(2)}, u32[]{:S(2)}) async-start(bf16[128,8,512]{2,0,1:T(8,128)(2,1)} %bitcast.231), calls=%async_computation.9 | async-start | bytes 2097152 | tf_op jit(solution)/shard_map/all_to_all | solution.py:130
  210.8 19.5 %all-to-all-start.1 = ((bf16[128,8,512]{2,0,1:T(8,128)(2,1)}), bf16[128,8,512]{2,0,1:T(8,128)(2,1)S(1)}, u32[]{:S(2)}, u32[]{:S(2)}) async-start(bf16[128,8,512]{2,0,1:T(8,128)(2,1)} %bitcast.189), calls=%async_computation.1 | async-start | bytes 2097152 | tf_op jit(solution)/shard_map/all_to_all | solution.py:127
  222.9 48.5 %copy-start.15 = (bf16[7,128,128]{2,1,0:T(8,128)(2,1)}, bf16[7,128,128]{2,1,0:T(8,128)(2,1)S(1)}, u32[]{:S(2)}) copy-start(bf16[7,128,128]{2,1,0:T(8,128)(2,1)S(1)} %slice.395) | copy-start | bytes 688132
  255.8 10.7 %copy-start.5 = (bf16[512,640]{1,0:T(8,128)(2,1)}, bf16[512,640]{1,0:T(8,128)(2,1)S(1)}, u32[]{:S(2)}) copy-start(bf16[512,640]{1,0:T(8,128)(2,1)S(1)} %multiply_convert_fusion.3) | copy-start | bytes 1966084
  287.4 11.6 %all-to-all-start.14 = ((bf16[8,128,128]{1,2,0:T(8,128)(2,1)}), bf16[8,128,128]{1,2,0:T(8,128)(2,1)}, u32[]{:S(2)}, u32[]{:S(2)}) async-start(bf16[8,128,128]{1,2,0:T(8,128)(2,1)} %copy.21), calls=%async_computation.14 | async-start | bytes 524288 | tf_op jit(solution)/shard_map/all_to_all | solution.py:141
  293.9 8.7 %copy-start.7 = (bf16[512,512]{0,1:T(8,128)(2,1)S(1)}, bf16[512,512]{0,1:T(8,128)(2,1)}, u32[]{:S(2)}) copy-start(bf16[512,512]{0,1:T(8,128)(2,1)} %copy-done.6) | copy-start | bytes 1572868
  298.9 11.1 %all-to-all-start.12 = ((bf16[8,128,128]{1,2,0:T(8,128)(2,1)}), bf16[8,128,128]{1,2,0:T(8,128)(2,1)S(1)}, u32[]{:S(2)}, u32[]{:S(2)}) async-start(bf16[8,128,128]{1,2,0:T(8,128)(2,1)} %copy.19), calls=%async_computation.12 | async-start | bytes 524288 | tf_op jit(solution)/shard_map/all_to_all | solution.py:138
  302.6 13.8 %copy-start.4 = (bf16[512,768]{1,0:T(8,128)(2,1)S(1)}, bf16[512,768]{1,0:T(8,128)(2,1)}, u32[]{:S(2)}) copy-start(bf16[512,768]{1,0:T(8,128)(2,1)} %copy-done.3) | copy-start | bytes 2359300
  303.6 14.7 %copy-start.2 = (bf16[512,896]{1,0:T(8,128)(2,1)S(1)}, bf16[512,896]{1,0:T(8,128)(2,1)}, u32[]{:S(2)}) copy-start(bf16[512,896]{1,0:T(8,128)(2,1)} %copy-done.1) | copy-start | bytes 2752516
  310.0 20.2 %all-to-all-start.6 = ((bf16[8,128,512]{1,2,0:T(8,128)(2,1)}), bf16[8,128,512]{1,2,0:T(8,128)(2,1)}, u32[]{:S(2)}, u32[]{:S(2)}) async-start(bf16[8,128,512]{1,2,0:T(8,128)(2,1)} %copy.14), calls=%async_computation.6 | async-start | bytes 2097152 | tf_op jit(solution)/shard_map/all_to_all | solution.py:136
  330.2 19.5 %all-to-all-start.10 = ((bf16[8,128,512]{1,2,0:T(8,128)(2,1)}), bf16[8,128,512]{1,2,0:T(8,128)(2,1)S(1)}, u32[]{:S(2)}, u32[]{:S(2)}) async-start(bf16[8,128,512]{1,2,0:T(8,128)(2,1)} %copy.17), calls=%async_computation.10 | async-start | bytes 2097152 | tf_op jit(solution)/shard_map/all_to_all | solution.py:137
  350.7 23.8 %all-to-all-start.15 = ((bf16[32,8,1024]{2,1,0:T(8,128)(2,1)}), bf16[32,8,1024]{2,1,0:T(8,128)(2,1)S(1)}, u32[]{:S(2)}, u32[]{:S(2)}) async-start(bf16[32,8,1024]{2,1,0:T(8,128)(2,1)} %bitcast.62), calls=%async_computation.15 | async-start | bytes 1048576 | tf_op jit(solution)/shard_map/all_to_all | solution.py:159
  374.5 21.8 %all-to-all-start.13 = ((bf16[32,8,1024]{2,1,0:T(8,128)(2,1)}), bf16[32,8,1024]{2,1,0:T(8,128)(2,1)S(1)}, u32[]{:S(2)}, u32[]{:S(2)}) async-start(bf16[32,8,1024]{2,1,0:T(8,128)(2,1)} %bitcast.57), calls=%async_computation.13 | async-start | bytes 1048576 | tf_op jit(solution)/shard_map/all_to_all | solution.py:152
  396.3 54.3 %all-to-all-start.7 = ((bf16[32,8,4096]{2,1,0:T(8,128)(2,1)}), bf16[32,8,4096]{2,1,0:T(8,128)(2,1)S(1)}, u32[]{:S(2)}, u32[]{:S(2)}) async-start(bf16[32,8,4096]{2,1,0:T(8,128)(2,1)} %bitcast.206), calls=%async_computation.7 | async-start | bytes 4194304 | tf_op jit(solution)/shard_map/all_to_all | solution.py:146
  450.5 55.8 %all-to-all-start.11 = ((bf16[32,8,4096]{2,1,0:T(8,128)(2,1)}), bf16[32,8,4096]{2,1,0:T(8,128)(2,1)}, u32[]{:S(2)}, u32[]{:S(2)}) async-start(bf16[32,8,4096]{2,1,0:T(8,128)(2,1)} %bitcast.205), calls=%async_computation.11 | async-start | bytes 4194304 | tf_op jit(solution)/shard_map/all_to_all | solution.py:149
  (46 other events, 115.1 us)
where the time goes:
time: 521 us; the launch traced here: 512 us
  waiting for transfers between devices  277 us (53%)
  local copies, waits for them, and re-layouts  89.6 us (17%)
  starting transfers between devices  81.9 us (16%)
  matrix products  51.4 us (10%)
  other arithmetic  9.73 us (2%)
    all_to_all x1, waiting for transfers between devices, per_device(): lax.all_to_all(pack_rows(out_grad, send_slot, total), 'grp', split_axis=0...  44.7 us
    all_to_all x1, waiting for transfers between devices, per_device(): lax.all_to_all(pack_rows(grad_query, recv_slot, total), 'grp', split_axis...  43.9 us
    all_to_all x1, waiting for transfers between devices, per_device(): lax.all_to_all(pack_rows(output, recv_slot, total), 'grp', split_axis=0,...  42.8 us
    all_to_all x1, waiting for transfers between devices, per_device(): lax.all_to_all(pack_rows(queries, send_slot, total), 'grp', split_axis=0,...  41.9 us
    scatter x8, local copies, waits for them, and re-layouts, pack_rows(): jnp.zeros((total, source_rows.shape[1]), source_rows.dtype).at[slots]  25.6 us
    all_to_all x1, waiting for transfers between devices, per_device(): lax.all_to_all(pack_rows(value_row_matrix, send_slot, total), 'grp', spli...  15.2 us
    all_to_all x1, waiting for transfers between devices, per_device(): lax.all_to_all(pack_rows(value_gradient_fn, recv_slot, total), 'grp', spl...  15.2 us
    all_to_all x1, waiting for transfers between devices, per_device(): lax.all_to_all(pack_rows(key_row_matrix, send_slot, total), 'grp', split_...  14.4 us
  transfers between devices with their start and end apart: 16, of which 16 were waited for; matrix products, arithmetic and copies ran while one was open for 16% of the time, Pallas kernels for 0%

commit v1 on v0

v1 whole, which is shorter than its diff:
```python
import math

import jax
import jax.numpy as jnp
from jax import lax
from jax.experimental import pallas as pl
from jax.experimental.pallas import tpu as pltpu
from jax.sharding import PartitionSpec as P

HEAD = 128
F32 = jnp.float32
BF16 = jnp.bfloat16
VMEM_BYTES = 56 * 1024 * 1024


def slot_tables(labels, capacity):
    count = labels.shape[1]
    across = jnp.broadcast_to(labels.astype(F32), (count, count))
    down = across.T
    i = lax.broadcasted_iota(jnp.int32, (count, count), 0)
    j = lax.broadcasted_iota(jnp.int32, (count, count), 1)
    same = across == down
    rank_row = jnp.sum(jnp.where(same & (i < j), 1.0, 0.0), axis=0, keepdims=True)
    rank_col = jnp.sum(jnp.where(same & (j < i), 1.0, 0.0), axis=1, keepdims=True)
    slot_row = across[:1, :] * capacity + rank_row
    slot_col = down[:, :1] * capacity + rank_col
    return slot_row.astype(jnp.int32), slot_col.astype(jnp.int32)


def one_hot_rows(slot_row, total):
    t = lax.broadcasted_iota(jnp.int32, (total, slot_row.shape[1]), 0)
    return jnp.where(t == slot_row, 1.0, 0.0).astype(BF16)


def one_hot_cols(slot_col, total):
    t = lax.broadcasted_iota(jnp.int32, (slot_col.shape[0], total), 1)
    return jnp.where(t == slot_col, 1.0, 0.0).astype(BF16)


def pick(marks, rows):
    return jnp.dot(marks, rows, preferred_element_type=F32).astype(BF16)


def pack_kernel(capacity, labels_ref, q_ref, g_ref, k_ref, v_ref, out_ref, marks_ref):
    total = out_ref.shape[1]

    @pl.when(pl.program_id(0) == 0)
    def _():
        slot_row, _ = slot_tables(labels_ref[...], capacity)
        marks_ref[...] = one_hot_rows(slot_row, total)

    rows = jnp.concatenate([q_ref[...], g_ref[...], k_ref[...], v_ref[...]], axis=1)
    out_ref[0] = pick(marks_ref[...], rows)


def unpack_kernel(capacity, labels_ref, got_ref, o_ref, dq_ref, dk_ref, dv_ref, marks_ref):
    total = got_ref.shape[1]
    wide = o_ref.shape[1]

    @pl.when(pl.program_id(0) == 0)
    def _():
        _, slot_col = slot_tables(labels_ref[...], capacity)
        marks_ref[...] = one_hot_cols(slot_col, total)

    rows = pick(marks_ref[...], got_ref[0])
    o_ref[...] = rows[:, :wide]
    dq_ref[...] = rows[:, wide : 2 * wide]
    dk_ref[...] = rows[:, 2 * wide : 2 * wide + HEAD]
    dv_ref[...] = rows[:, 2 * wide + HEAD :]


def attend_kernel(
    capacity, got_ref, source_ref, start_ref, out_ref, x_ref, y_ref, kt_ref, vt_ref, dk_ref, dv_ref
):
    columns, total, width = got_ref.shape
    tok = source_ref.shape[1]
    share = (width - 2 * HEAD) // (2 * HEAD)
    wide = share * HEAD
    scaling = 1.0 / math.sqrt(HEAD)
    power_scale = scaling * math.log2(math.e)
    across = (((1,), (1,)), ((), ()))
    k_cols = slice(2 * wide, 2 * wide + HEAD)
    v_cols = slice(2 * wide + HEAD, 2 * wide + 2 * HEAD)
    slots = [slot_tables(source_ref[s : s + 1, :], capacity) for s in range(columns)]
    for s in range(columns):
        x_ref[s * tok : (s + 1) * tok, :] = pick(one_hot_cols(slots[s][1], total), got_ref[s])
    kt_ref[...] = x_ref[:, k_cols].astype(F32).T.astype(BF16)
    vt_ref[...] = x_ref[:, v_cols].astype(F32).T.astype(BF16)
    dk_ref[...] = jnp.zeros(dk_ref.shape, F32)
    dv_ref[...] = jnp.zeros(dv_ref.shape, F32)
    joint = 2 if share % 2 == 0 else 1
    for s in range(columns):
        rows = slice(s * tok, (s + 1) * tok)
        seen = (s + 1) * tok
        place = lax.broadcasted_iota(jnp.int32, (seen, tok), 0)
        own = s * tok + lax.broadcasted_iota(jnp.int32, (seen, tok), 1)
        visible = (place >= start_ref[:, rows]) & (place <= own)
        visible = jnp.concatenate([visible.astype(F32)] * joint, axis=1) > 0.5
        for first in range(0, share, joint):
            heads = range(first, first + joint)
            q = jnp.concatenate([x_ref[rows, h * HEAD : (h + 1) * HEAD] for h in heads], axis=0)
            g = jnp.concatenate(
                [x_ref[rows, wide + h * HEAD : wide + (h + 1) * HEAD] for h in heads], axis=0
            )
            k = x_ref[:seen, k_cols]
            v = x_ref[:seen, v_cols]
            scores = lax.dot_general(k, q, across, preferred_element_type=F32)
            scores = jnp.where(visible, scores * power_scale, -jnp.inf)
            powers = jnp.exp2(scores - jnp.max(scores, axis=0, keepdims=True))
            prob = powers * (1.0 / jnp.sum(powers, axis=0, keepdims=True))
            weights = prob.astype(BF16)
            prob_grad = lax.dot_general(v, g, across, preferred_element_type=F32)
            spread = jnp.sum(prob * prob_grad, axis=0, keepdims=True)
            dscore = (prob * (prob_grad - spread) * scaling).astype(BF16)
            o_t = jnp.dot(vt_ref[:, :seen], weights, preferred_element_type=F32)
            dq_t = jnp.dot(kt_ref[:, :seen], dscore, preferred_element_type=F32)
            dk_ref[:seen, :] += jnp.dot(dscore, q, preferred_element_type=F32)
            dv_ref[:seen, :] += jnp.dot(weights, g, preferred_element_type=F32)
            for n, h in enumerate(heads):
                part = slice(n * tok, (n + 1) * tok)
                y_ref[rows, h * HEAD : (h + 1) * HEAD] = o_t[:, part].T.astype(BF16)
                y_ref[rows, wide + h * HEAD : wide + (h + 1) * HEAD] = dq_t[:, part].T.astype(BF16)
    y_ref[:, k_cols] = dk_ref[...].astype(BF16)
    y_ref[:, v_cols] = dv_ref[...].astype(BF16)
    for s in range(columns):
        out_ref[s] = pick(one_hot_rows(slots[s][0], total), y_ref[s * tok : (s + 1) * tok, :])


def params():
    return pltpu.CompilerParams(vmem_limit_bytes=VMEM_BYTES)


def pack(labels, queries, grads, keys, values, columns, total, capacity):
    tok = queries.shape[0]
    wide = queries.shape[1] // columns
    narrow = keys.shape[1] // columns
    width = 2 * (wide + narrow)

    def part(size):
        return pl.BlockSpec((tok, size), lambda c: (0, c))

    return pl.pallas_call(
        lambda *refs: pack_kernel(capacity, *refs),
        grid=(columns,),
        in_specs=[
            pl.BlockSpec((1, tok), lambda c: (0, 0)),
            part(wide),
            part(wide),
            part(narrow),
            part(narrow),
        ],
        out_specs=pl.BlockSpec((1, total, width), lambda c: (c, 0, 0)),
        out_shape=jax.ShapeDtypeStruct((columns, total, width), BF16),
        scratch_shapes=[pltpu.VMEM((total, tok), BF16)],
        compiler_params=params(),
        name="pack_rows",
    )(labels, queries, grads, keys, values)


def unpack(labels, got, wide, capacity):
    columns, total, width = got.shape
    tok = labels.shape[1]

    def part(size):
        return pl.BlockSpec((tok, size), lambda c: (0, c))

    return pl.pallas_call(
        lambda *refs: unpack_kernel(capacity, *refs),
        grid=(columns,),
        in_specs=[
            pl.BlockSpec((1, tok), lambda c: (0, 0)),
            pl.BlockSpec((1, total, width), lambda c: (c, 0, 0)),
        ],
        out_specs=[part(wide), part(wide), part(HEAD), part(HEAD)],
        out_shape=[
            jax.ShapeDtypeStruct((tok, columns * size), BF16) for size in (wide, wide, HEAD, HEAD)
        ],
        scratch_shapes=[pltpu.VMEM((tok, total), BF16)],
        compiler_params=params(),
        name="unpack_rows",
    )(labels, got)


def attend(got, sources, starts, capacity):
    columns, total, width = got.shape
    rows = starts.shape[1]
    return pl.pallas_call(
        lambda *refs: attend_kernel(capacity, *refs),
        out_shape=jax.ShapeDtypeStruct(got.shape, BF16),
        scratch_shapes=[
            pltpu.VMEM((rows, width), BF16),
            pltpu.VMEM((rows, width), BF16),
            pltpu.VMEM((HEAD, rows), BF16),
            pltpu.VMEM((HEAD, rows), BF16),
            pltpu.VMEM((rows, HEAD), F32),
            pltpu.VMEM((rows, HEAD), F32),
        ],
        compiler_params=params(),
        name="attend_group",
    )(got, sources, starts)


def swap(rows, columns, groups):
    _, total, width = rows.shape
    blocks = rows.reshape(columns * groups, total // groups, width)
    moved = lax.all_to_all(blocks, ("sp", "grp"), split_axis=0, concat_axis=0, tiled=True)
    return moved.reshape(columns, total, width)


def per_device(
    queries, key_row_matrix, value_row_matrix, out_grad, dest_group, source_group, seq_start
):
    groups = lax.axis_size("grp")
    columns = lax.axis_size("sp")
    tok = queries.shape[0]
    capacity = 2 * tok // groups
    total = groups * capacity
    wide = queries.shape[1] // columns
    with jax.named_scope("pack"):
        sent = pack(
            dest_group, queries, out_grad, key_row_matrix, value_row_matrix, columns, total, capacity
        )
    with jax.named_scope("tables"):
        sources = lax.all_gather(source_group, "sp", axis=0, tiled=True)
    with jax.named_scope("to_groups"):
        got = swap(sent, columns, groups)
    with jax.named_scope("attend"):
        done = attend(got, sources, seq_start, capacity)
    with jax.named_scope("to_homes"):
        back = swap(done, columns, groups)
    with jax.named_scope("unpack"):
        return tuple(unpack(dest_group, back, wide, capacity))


def solution(mesh):
    rows = P(("grp", "sp"), None)
    table = P("grp", "sp")
    return jax.shard_map(
        per_device,
        mesh=mesh,
        in_specs=(rows, rows, rows, rows, table, table, P("grp", None)),
        out_specs=(rows, rows, rows, rows),
        check_vma=False,
    )
```

time: 521 us -> 300 us (0.58); the launches traced: 512 us -> 299 us
  waiting for transfers between devices: 277 us -> 103 us
  blocking collectives: 0 us -> 145 us
  local copies, waits for them, and re-layouts: 89.6 us -> 0.01 us
  starting transfers between devices: 81.9 us -> 15.3 us
  matrix products: 51.4 us -> 0 us
  Pallas kernels: 0 us -> 35.7 us
  other arithmetic: 9.73 us -> 0 us
    all_to_all x16 -> x1, waiting for transfers between devices: 277 us -> 103 us  [swap(): lax.all_to_all(blocks, ('sp', 'grp'), split_axis=0, concat_axis=0, tiled=...]
    all_to_all x0 -> x1, blocking collectives: none -> 128 us  [swap(): lax.all_to_all(blocks, ('sp', 'grp'), split_axis=0, concat_axis=0, tiled=...]
    all_to_all x16 -> x1, starting transfers between devices: 81.9 us -> 15.3 us  [swap(): lax.all_to_all(blocks, ('sp', 'grp'), split_axis=0, concat_axis=0, tiled=...]
    dot_general x48 -> x0, matrix products: 51.4 us -> none  [the longest x8 13.7 us: head_block(): lax.dot_general(query_part, key_part, across, preferred_element_type=jnp....]
    pallas_call x0 -> x3, Pallas kernels: none -> 35.7 us  [the longest x1 20.8 us: attend(): pl.pallas_call(lambda *refs: attend_kernel(capacity, *refs), out_shape=ja...]
    scatter x8 -> x0, local copies, waits for them, and re-layouts: 25.6 us -> none  [pack_rows(): jnp.zeros((total, source_rows.shape[1]), source_rows.dtype).at[slots]]
    gather x8 -> x0, local copies, waits for them, and re-layouts: 19.2 us -> none  [the longest x1 5.04 us: per_device(): grad_seq = arrived[3][recv_slot]]
    all_to_all x14 -> x0, local copies, waits for them, and re-layouts: 18.8 us -> none  [the longest x3 5.27 us: per_device(): lax.all_to_all(grad_query, 'sp', split_axis=0, concat_axis=1, tiled=True)]
  transfers between devices with their start and end apart: 16 -> 1, of which waited for: 16 -> 1; matrix products, arithmetic and copies ran while one was open for 16% -> 0% of each run, Pallas kernels for 0% -> 0%
where the time goes in v1:
time: 300 us; the launch traced here: 299 us
  blocking collectives  145 us (48%)
  waiting for transfers between devices  103 us (34%)
  Pallas kernels  35.7 us (12%)
  starting transfers between devices  15.3 us (5%)
    all_to_all x1, blocking collectives, swap(): lax.all_to_all(blocks, ('sp', 'grp'), split_axis=0, concat_axis=0, tiled=...  128 us
    all_to_all x1, waiting for transfers between devices, swap(): lax.all_to_all(blocks, ('sp', 'grp'), split_axis=0, concat_axis=0, tiled=...  103 us
    pallas_call x1, Pallas kernels, attend(): pl.pallas_call(lambda *refs: attend_kernel(capacity, *refs), out_shape=ja...  20.8 us
    all_gather x1, blocking collectives, per_device(): sources = lax.all_gather(source_group, 'sp', axis=0, tiled=True)  16.7 us
    all_to_all x1, starting transfers between devices, swap(): lax.all_to_all(blocks, ('sp', 'grp'), split_axis=0, concat_axis=0, tiled=...  15.3 us
    pallas_call x1, Pallas kernels, pack(): pl.pallas_call(lambda *refs: pack_kernel(capacity, *refs), grid=(columns,...  7.63 us
    pallas_call x1, Pallas kernels, unpack(): pl.pallas_call(lambda *refs: unpack_kernel(capacity, *refs), grid=(column...  7.25 us
  transfers between devices with their start and end apart: 1, of which 1 were waited for; matrix products, arithmetic and copies ran while one was open for 0% of the time, Pallas kernels for 0%

profile of v1, /device:TPU:32, one launch (start us, length us, event | category | flops | bytes accessed | tf_op | source)
XLA Modules:
  0.0 298.8 jit_solution(14823045656310593100)
XLA Ops:
  0.6 7.6 %pack_rows.1 = bf16[8,256,1280]{2,1,0:T(8,128)(2,1)} custom-call(s32[1,128]{1,0:T(1,128)} %refs_0_.3, bf16[128,4096]{1,0:T(8,128)(2,1)} %refs_1_.1, bf16[128,4096]{1,0:T(8,128)(2,1)} %refs_2_.2, bf16[128,1024]{1,0:T(8,128)(2,1)} %refs_3_.1, bf16[128,1024]{1,0:T(8,128)(2,1)} %refs_4_.1), custom_call_target="tpu_custom_call" | custom-call | tf_op jit(solution)/shard_map/pack/pack_rows/pallas_call | solution.py:142
  8.3 0.0 copy-start
  8.3 15.3 %all-to-all-start = ((bf16[256,8,1280]{2,1,0:T(8,128)(2,1)}), bf16[256,8,1280]{2,1,0:T(8,128)(2,1)}, u32[]{:S(2)}, u32[]{:S(2)}) async-start(bf16[256,8,1280]{2,1,0:T(8,128)(2,1)} %bitcast.6), calls=%async_computation | async-start | bytes 10485760 | tf_op jit(solution)/shard_map/to_groups/all_to_all | solution.py:206
  23.5 0.0 copy-done
  23.5 16.7 %all-gather = s32[8,1,128]{2,1,0:T(1,128)} all-gather(s32[1,1,128]{2,1,0:T(1,128)S(1)} %bitcast.10), channel_id=1, replica_groups=mesh['grp'=32,'sp'=8] {'sp'}, dimensions={0}, use_global_device_ids=true | all-gather | bytes 4608 | tf_op jit(solution)/shard_map/tables/all_gather | solution.py:224
  40.3 102.6 %all-to-all-done = bf16[256,8,1280]{2,1,0:T(8,128)(2,1)} async-done(((bf16[256,8,1280]{2,1,0:T(8,128)(2,1)}), bf16[256,8,1280]{2,1,0:T(8,128)(2,1)}, u32[]{:S(2)}, u32[]{:S(2)}) %all-to-all-start) | async-done | bytes 5242912 | tf_op jit(solution)/shard_map/to_groups/all_to_all | solution.py:206
  142.8 20.8 %attend_group.1 = bf16[8,256,1280]{2,1,0:T(8,128)(2,1)} custom-call(bf16[8,256,1280]{2,1,0:T(8,128)(2,1)} %bitcast.1.refs_0_, s32[8,128]{1,0:T(8,128)} %bitcast.9, s32[1,1024]{1,0:T(1,128)} %refs_2_.3), custom_call_target="tpu_custom_call" | custom-call | tf_op jit(solution)/shard_map/attend/attend_group/pallas_call | solution.py:187
  163.7 127.8 %all_to_all.10 = bf16[256,8,1280]{2,1,0:T(8,128)(2,1)} all-to-all(bf16[256,8,1280]{2,1,0:T(8,128)(2,1)} %bitcast.8), channel_id=1, replica_groups=mesh['grp'=32,'sp'=8] {'sp','grp'}, dimensions={0} | all-to-all | bytes 10485760 | tf_op jit(solution)/shard_map/to_homes/all_to_all | solution.py:206
  291.5 7.2 %unpack_rows.1 = (bf16[128,4096]{1,0:T(8,128)(2,1)}, bf16[128,4096]{1,0:T(8,128)(2,1)}, bf16[128,1024]{1,0:T(8,128)(2,1)}, bf16[128,1024]{1,0:T(8,128)(2,1)}) custom-call(s32[1,128]{1,0:T(1,128)} %refs_0_.3, bf16[8,256,1280]{2,1,0:T(8,128)(2,1)} %bitcast.7), custom_call_target="tpu_custom_call" | custom-call | tf_op jit(solution)/shard_map/unpack/unpack_rows/pallas_call | solution.py:167
Async XLA Ops:
  8.3 15.3 %copy-start = (s32[1,128]{1,0:T(1,128)S(1)}, s32[1,128]{1,0:T(1,128)}, u32[]{:S(2)}) copy-start(s32[1,128]{1,0:T(1,128)} %param.12) | copy-start | bytes 1540
  8.3 134.6 %all-to-all-start = ((bf16[256,8,1280]{2,1,0:T(8,128)(2,1)}), bf16[256,8,1280]{2,1,0:T(8,128)(2,1)}, u32[]{:S(2)}, u32[]{:S(2)}) async-start(bf16[256,8,1280]{2,1,0:T(8,128)(2,1)} %bitcast.6), calls=%async_computation | async-start | bytes 10485760 | tf_op jit(solution)/shard_map/to_groups/all_to_all | solution.py:206

commit v2 on v1

v2 whole, which is shorter than its diff:
```python
import math

import jax
import jax.numpy as jnp
from jax import lax
from jax.experimental import pallas as pl
from jax.experimental.pallas import tpu as pltpu
from jax.sharding import PartitionSpec as P

HEAD = 128
F32 = jnp.float32
BF16 = jnp.bfloat16
VMEM_BYTES = 56 * 1024 * 1024


def slot_tables(labels, capacity):
    count = labels.shape[1]
    across = jnp.broadcast_to(labels.astype(F32), (count, count))
    down = across.T
    i = lax.broadcasted_iota(jnp.int32, (count, count), 0)
    j = lax.broadcasted_iota(jnp.int32, (count, count), 1)
    same = across == down
    rank_row = jnp.sum(jnp.where(same & (i < j), 1.0, 0.0), axis=0, keepdims=True)
    rank_col = jnp.sum(jnp.where(same & (j < i), 1.0, 0.0), axis=1, keepdims=True)
    slot_row = across[:1, :] * capacity + rank_row
    slot_col = down[:, :1] * capacity + rank_col
    return slot_row.astype(jnp.int32), slot_col.astype(jnp.int32)


def one_hot_rows(slot_row, total):
    t = lax.broadcasted_iota(jnp.int32, (total, slot_row.shape[1]), 0)
    return jnp.where(t == slot_row, 1.0, 0.0).astype(BF16)


def one_hot_cols(slot_col, total):
    t = lax.broadcasted_iota(jnp.int32, (slot_col.shape[0], total), 1)
    return jnp.where(t == slot_col, 1.0, 0.0).astype(BF16)


def pick(marks, rows):
    return jnp.dot(marks, rows, preferred_element_type=F32).astype(BF16)


def pack_kernel(
    capacity, labels_ref, q_hbm, g_hbm, k_hbm, v_hbm, out_hbm, q_ref, g_ref, k_ref, v_ref, out_ref, in_sem, out_sem
):
    columns, total, _ = out_ref.shape
    wide = q_ref.shape[1] // columns
    narrow = k_ref.shape[1] // columns

    def column(c):
        pairs = ((q_hbm, q_ref, wide), (g_hbm, g_ref, wide), (k_hbm, k_ref, narrow), (v_hbm, v_ref, narrow))
        return [
            pltpu.make_async_copy(
                src.at[:, pl.ds(c * size, size)], dst.at[:, pl.ds(c * size, size)], in_sem.at[n, c]
            )
            for n, (src, dst, size) in enumerate(pairs)
        ]

    def leave(c):
        return pltpu.make_async_copy(out_ref.at[c], out_hbm.at[c], out_sem.at[c])

    for c in range(columns):
        for copy in column(c):
            copy.start()
    slot_row, _ = slot_tables(labels_ref[...], capacity)
    marks = one_hot_rows(slot_row, total)
    for c in range(columns):
        for copy in column(c):
            copy.wait()
        w = slice(c * wide, (c + 1) * wide)
        n = slice(c * narrow, (c + 1) * narrow)
        out_ref[c, :, :wide] = pick(marks, q_ref[:, w])
        out_ref[c, :, wide : 2 * wide] = pick(marks, g_ref[:, w])
        out_ref[c, :, 2 * wide :] = pick(marks, jnp.concatenate([k_ref[:, n], v_ref[:, n]], axis=1))
        leave(c).start()
    for c in range(columns):
        leave(c).wait()


def unpack_kernel(
    capacity, labels_ref, got_hbm, o_hbm, dq_hbm, dk_hbm, dv_hbm, got_ref, o_ref, dq_ref, dk_ref, dv_ref, in_sem, out_sem
):
    columns, total, _ = got_ref.shape
    wide = o_ref.shape[1] // columns
    narrow = dk_ref.shape[1] // columns

    def arrive(c):
        return pltpu.make_async_copy(got_hbm.at[c], got_ref.at[c], in_sem.at[c])

    def column(c):
        pairs = ((o_ref, o_hbm, wide), (dq_ref, dq_hbm, wide), (dk_ref, dk_hbm, narrow), (dv_ref, dv_hbm, narrow))
        return [
            pltpu.make_async_copy(
                src.at[:, pl.ds(c * size, size)], dst.at[:, pl.ds(c * size, size)], out_sem.at[n, c]
            )
            for n, (src, dst, size) in enumerate(pairs)
        ]

    for c in range(columns):
        arrive(c).start()
    _, slot_col = slot_tables(labels_ref[...], capacity)
    marks = one_hot_cols(slot_col, total)
    for c in range(columns):
        arrive(c).wait()
        w = slice(c * wide, (c + 1) * wide)
        n = slice(c * narrow, (c + 1) * narrow)
        o_ref[:, w] = pick(marks, got_ref[c, :, :wide])
        dq_ref[:, w] = pick(marks, got_ref[c, :, wide : 2 * wide])
        rest = pick(marks, got_ref[c, :, 2 * wide :])
        dk_ref[:, n] = rest[:, :narrow]
        dv_ref[:, n] = rest[:, narrow:]
        for copy in column(c):
            copy.start()
    for c in range(columns):
        for copy in column(c):
            copy.wait()


def attend_kernel(
    capacity, source_ref, start_ref, got_hbm, out_hbm, got_ref, out_ref, x_ref, s_ref, p_ref, pg_ref, w_ref, ds_ref,
    kt_ref, vt_ref, dk_ref, dv_ref, in_sem, out_sem, last_sem,
):
    columns, total, width = got_ref.shape
    tok = source_ref.shape[1]
    share = (width - 2 * HEAD) // (2 * HEAD)
    wide = share * HEAD
    scaling = 1.0 / math.sqrt(HEAD)
    power_scale = scaling * math.log2(math.e)
    across = (((1,), (1,)), ((), ()))
    k_cols = slice(2 * wide, 2 * wide + HEAD)
    v_cols = slice(2 * wide + HEAD, 2 * wide + 2 * HEAD)
    joint = 2
    lanes = joint * tok

    def arrive(s):
        return pltpu.make_async_copy(got_hbm.at[s], got_ref.at[s], in_sem.at[s])

    def leave(s):
        cols = pl.ds(0, 2 * wide)
        return pltpu.make_async_copy(out_ref.at[s, :, cols], out_hbm.at[s, :, cols], out_sem.at[s])

    def leave_last(s):
        cols = pl.ds(2 * wide, 2 * HEAD)
        return pltpu.make_async_copy(out_ref.at[s, :, cols], out_hbm.at[s, :, cols], last_sem.at[s])

    def fold(values, op):
        return op(values.reshape(tok // 8, 8, lanes), axis=0)

    for s in range(columns):
        arrive(s).start()
    slots = [slot_tables(source_ref[s : s + 1, :], capacity) for s in range(columns)]
    place = lax.broadcasted_iota(jnp.int32, (tok, lanes), 0)
    lane = lax.broadcasted_iota(jnp.int32, (tok, lanes), 1) % tok
    for s in range(columns):
        rows = slice(s * tok, (s + 1) * tok)
        seen = (s + 1) * tok
        arrive(s).wait()
        x_ref[rows, :] = pick(one_hot_cols(slots[s][1], total), got_ref[s])
        kt_ref[:, rows] = x_ref[rows, k_cols].astype(F32).T.astype(BF16)
        vt_ref[:, rows] = x_ref[rows, v_cols].astype(F32).T.astype(BF16)
        start = jnp.concatenate([start_ref[:, rows]] * joint, axis=1)
        for first in range(0, share, joint):
            heads = range(first, first + joint)
            part = slice(first * tok, first * tok + lanes)
            q = jnp.concatenate([x_ref[rows, h * HEAD : (h + 1) * HEAD] for h in heads], axis=0)
            g = jnp.concatenate(
                [x_ref[rows, wide + h * HEAD : wide + (h + 1) * HEAD] for h in heads], axis=0
            )
            top = None
            for t in range(s + 1):
                keys = slice(t * tok, (t + 1) * tok)
                scores = lax.dot_general(x_ref[keys, k_cols], q, across, preferred_element_type=F32)
                visible = place >= start - t * tok
                if t == s:
                    visible = visible & (place <= lane)
                scores = jnp.where(visible, scores, -jnp.inf)
                s_ref[keys, :] = scores
                best = fold(scores, jnp.max)
                top = best if top is None else jnp.maximum(top, best)
            top = jnp.max(top, axis=0, keepdims=True)
            mass = jnp.zeros((8, lanes), F32)
            spread = jnp.zeros((8, lanes), F32)
            for t in range(s + 1):
                keys = slice(t * tok, (t + 1) * tok)
                powers = jnp.exp2((s_ref[keys, :] - top) * power_scale)
                prob_grad = lax.dot_general(x_ref[keys, v_cols], g, across, preferred_element_type=F32)
                p_ref[keys, :] = powers
                pg_ref[keys, :] = prob_grad
                mass = mass + fold(powers, jnp.sum)
                spread = spread + fold(powers * prob_grad, jnp.sum)
            inverse = 1.0 / jnp.sum(mass, axis=0, keepdims=True)
            spread = jnp.sum(spread, axis=0, keepdims=True) * inverse
            scaled = inverse * scaling
            for t in range(s + 1):
                keys = slice(t * tok, (t + 1) * tok)
                powers = p_ref[keys, :]
                w_ref[keys, part] = (powers * inverse).astype(BF16)
                ds_ref[keys, part] = ((powers * scaled) * (pg_ref[keys, :] - spread)).astype(BF16)
        weights = w_ref[:seen, :]
        dscore = ds_ref[:seen, :]
        q = jnp.concatenate([x_ref[rows, h * HEAD : (h + 1) * HEAD] for h in range(share)], axis=0)
        g = jnp.concatenate(
            [x_ref[rows, wide + h * HEAD : wide + (h + 1) * HEAD] for h in range(share)], axis=0
        )
        marks = one_hot_rows(slots[s][0], total)
        for base, turned, pairs in ((0, vt_ref, weights), (wide, kt_ref, dscore)):
            result = jnp.dot(turned[:, :seen], pairs, preferred_element_type=F32).astype(BF16)
            stacked = jnp.concatenate([result[:, h * tok : (h + 1) * tok] for h in range(share)], axis=0)
            out_ref[s, :, base : base + wide] = lax.dot_general(
                marks, stacked, across, preferred_element_type=F32
            ).astype(BF16)
        leave(s).start()
        for total_ref, pairs, others in ((dk_ref, dscore, q), (dv_ref, weights, g)):
            result = jnp.dot(pairs, others, preferred_element_type=F32)
            if s:
                total_ref[: s * tok, :] += result[: s * tok]
            total_ref[rows, :] = result[s * tok :]
    for s in range(columns):
        rows = slice(s * tok, (s + 1) * tok)
        last = jnp.concatenate([dk_ref[rows, :], dv_ref[rows, :]], axis=1).astype(BF16)
        out_ref[s, :, 2 * wide :] = pick(one_hot_rows(slots[s][0], total), last)
        leave_last(s).start()
    for s in range(columns):
        leave(s).wait()
        leave_last(s).wait()


def params():
    return pltpu.CompilerParams(vmem_limit_bytes=VMEM_BYTES)


def pack(labels, queries, grads, keys, values, columns, total, capacity):
    width = 2 * (queries.shape[1] + keys.shape[1]) // columns
    far = pl.BlockSpec(memory_space=pl.ANY)
    return pl.pallas_call(
        lambda *refs: pack_kernel(capacity, *refs),
        in_specs=[pl.BlockSpec(memory_space=pltpu.VMEM), far, far, far, far],
        out_specs=far,
        out_shape=jax.ShapeDtypeStruct((columns, total, width), BF16),
        scratch_shapes=[
            pltpu.VMEM(queries.shape, BF16),
            pltpu.VMEM(grads.shape, BF16),
            pltpu.VMEM(keys.shape, BF16),
            pltpu.VMEM(values.shape, BF16),
            pltpu.VMEM((columns, total, width), BF16),
            pltpu.SemaphoreType.DMA((4, columns)),
            pltpu.SemaphoreType.DMA((columns,)),
        ],
        compiler_params=params(),
        name="pack_rows",
    )(labels, queries, grads, keys, values)


def unpack(labels, got, wide, capacity):
    columns, _, _ = got.shape
    tok = labels.shape[1]
    far = pl.BlockSpec(memory_space=pl.ANY)
    shapes = [(tok, columns * size) for size in (wide, wide, HEAD, HEAD)]
    return pl.pallas_call(
        lambda *refs: unpack_kernel(capacity, *refs),
        in_specs=[pl.BlockSpec(memory_space=pltpu.VMEM), far],
        out_specs=[far] * 4,
        out_shape=[jax.ShapeDtypeStruct(shape, BF16) for shape in shapes],
        scratch_shapes=[
            pltpu.VMEM(got.shape, BF16),
            *[pltpu.VMEM(shape, BF16) for shape in shapes],
            pltpu.SemaphoreType.DMA((columns,)),
            pltpu.SemaphoreType.DMA((4, columns)),
        ],
        compiler_params=params(),
        name="unpack_rows",
    )(labels, got)


def attend(got, sources, starts, capacity):
    columns, total, width = got.shape
    tok = sources.shape[1]
    rows = starts.shape[1]
    pairs = (width - 2 * HEAD) // (2 * HEAD) * tok
    near = pl.BlockSpec(memory_space=pltpu.VMEM)
    far = pl.BlockSpec(memory_space=pl.ANY)
    return pl.pallas_call(
        lambda *refs: attend_kernel(capacity, *refs),
        in_specs=[near, near, far],
        out_specs=far,
        out_shape=jax.ShapeDtypeStruct(got.shape, BF16),
        scratch_shapes=[
            pltpu.VMEM(got.shape, BF16),
            pltpu.VMEM(got.shape, BF16),
            pltpu.VMEM((rows, width), BF16),
            pltpu.VMEM((rows, 2 * tok), F32),
            pltpu.VMEM((rows, 2 * tok), F32),
            pltpu.VMEM((rows, 2 * tok), F32),
            pltpu.VMEM((rows, pairs), BF16),
            pltpu.VMEM((rows, pairs), BF16),
            pltpu.VMEM((HEAD, rows), BF16),
            pltpu.VMEM((HEAD, rows), BF16),
            pltpu.VMEM((rows, HEAD), F32),
            pltpu.VMEM((rows, HEAD), F32),
            pltpu.SemaphoreType.DMA((columns,)),
            pltpu.SemaphoreType.DMA((columns,)),
            pltpu.SemaphoreType.DMA((columns,)),
        ],
        compiler_params=params(),
        name="attend_group",
    )(sources, starts, got)


def swap(rows, columns, groups):
    _, total, width = rows.shape
    blocks = rows.reshape(columns * groups, total // groups, width)
    moved = lax.all_to_all(blocks, ("sp", "grp"), split_axis=0, concat_axis=0, tiled=True)
    return moved.reshape(columns, total, width)


def per_device(
    queries, key_row_matrix, value_row_matrix, out_grad, dest_group, source_group, seq_start
):
    groups = lax.axis_size("grp")
    columns = lax.axis_size("sp")
    tok = queries.shape[0]
    capacity = 2 * tok // groups
    total = groups * capacity
    wide = queries.shape[1] // columns
    with jax.named_scope("pack"):
        sent = pack(
            dest_group, queries, out_grad, key_row_matrix, value_row_matrix, columns, total, capacity
        )
    with jax.named_scope("tables"):
        sources = lax.all_gather(source_group, "sp", axis=0, tiled=True)
    with jax.named_scope("to_groups"):
        got = swap(sent, columns, groups)
    with jax.named_scope("attend"):
        done = attend(got, sources, seq_start, capacity)
    with jax.named_scope("to_homes"):
        back = swap(done, columns, groups)
    with jax.named_scope("unpack"):
        return tuple(unpack(dest_group, back, wide, capacity))


def solution(mesh):
    rows = P(("grp", "sp"), None)
    table = P("grp", "sp")
    return jax.shard_map(
        per_device,
        mesh=mesh,
        in_specs=(rows, rows, rows, rows, table, table, P("grp", None)),
        out_specs=(rows, rows, rows, rows),
        check_vma=False,
    )
```

time: 300 us -> 294 us (0.980)
  Pallas kernels: 35.7 us -> 29.7 us
    pallas_call x3, Pallas kernels: 35.7 us -> 29.7 us  [the longest x1 19.2 us: attend(): pl.pallas_call(lambda *refs: attend_kernel(capacity, *refs), in_specs=[ne...]
where the time goes in v2:
time: 294 us; the launch traced here: 293 us
  blocking collectives  145 us (49%)
  waiting for transfers between devices  103 us (35%)
  Pallas kernels  29.7 us (10%)
  starting transfers between devices  15.3 us (5%)
    all_to_all x1, blocking collectives, swap(): lax.all_to_all(blocks, ('sp', 'grp'), split_axis=0, concat_axis=0, tiled=...  128 us
    all_to_all x1, waiting for transfers between devices, swap(): lax.all_to_all(blocks, ('sp', 'grp'), split_axis=0, concat_axis=0, tiled=...  103 us
    pallas_call x1, Pallas kernels, attend(): pl.pallas_call(lambda *refs: attend_kernel(capacity, *refs), in_specs=[ne...  19.2 us
    all_gather x1, blocking collectives, per_device(): sources = lax.all_gather(source_group, 'sp', axis=0, tiled=True)  16.7 us
    all_to_all x1, starting transfers between devices, swap(): lax.all_to_all(blocks, ('sp', 'grp'), split_axis=0, concat_axis=0, tiled=...  15.3 us
  transfers between devices with their start and end apart: 1, of which 1 were waited for; matrix products, arithmetic and copies ran while one was open for 0% of the time, Pallas kernels for 0%

profile of v2, /device:TPU:32, one launch (start us, length us, event | category | flops | bytes accessed | tf_op | source)
XLA Modules:
  0.0 293.0 jit_solution(7507923372169089423)
XLA Ops:
  0.6 5.7 %pack_rows.1 = bf16[8,256,1280]{2,1,0:T(8,128)(2,1)} custom-call(s32[1,128]{1,0:T(1,128)} %refs_0_.3, bf16[128,4096]{1,0:T(8,128)(2,1)} %refs_1_.2, bf16[128,4096]{1,0:T(8,128)(2,1)} %refs_2_.1, bf16[128,1024]{1,0:T(8,128)(2,1)} %refs_3_.1, bf16[128,1024]{1,0:T(8,128)(2,1)} %refs_4_.1), custom_call_target="tpu_custom_call" | custom-call | tf_op jit(solution)/shard_map/pack/pack_rows/pallas_call | solution.py:236
  6.3 0.0 copy-start
  6.3 15.3 %all-to-all-start = ((bf16[256,8,1280]{2,1,0:T(8,128)(2,1)}), bf16[256,8,1280]{2,1,0:T(8,128)(2,1)}, u32[]{:S(2)}, u32[]{:S(2)}) async-start(bf16[256,8,1280]{2,1,0:T(8,128)(2,1)} %bitcast.6), calls=%async_computation | async-start | bytes 10485760 | tf_op jit(solution)/shard_map/to_groups/all_to_all | solution.py:313
  21.6 0.0 copy-done
  21.6 16.7 %all-gather = s32[8,1,128]{2,1,0:T(1,128)} all-gather(s32[1,1,128]{2,1,0:T(1,128)S(1)} %bitcast.10), channel_id=1, replica_groups=mesh['grp'=32,'sp'=8] {'sp'}, dimensions={0}, use_global_device_ids=true | all-gather | bytes 4608 | tf_op jit(solution)/shard_map/tables/all_gather | solution.py:331
  38.4 102.6 %all-to-all-done = bf16[256,8,1280]{2,1,0:T(8,128)(2,1)} async-done(((bf16[256,8,1280]{2,1,0:T(8,128)(2,1)}), bf16[256,8,1280]{2,1,0:T(8,128)(2,1)}, u32[]{:S(2)}, u32[]{:S(2)}) %all-to-all-start) | async-done | bytes 5242912 | tf_op jit(solution)/shard_map/to_groups/all_to_all | solution.py:313
  140.9 19.2 %attend_group.1 = bf16[8,256,1280]{2,1,0:T(8,128)(2,1)} custom-call(s32[8,128]{1,0:T(8,128)} %bitcast.9, s32[1,1024]{1,0:T(1,128)} %refs_1_.3, bf16[8,256,1280]{2,1,0:T(8,128)(2,1)} %bitcast.3.refs_2_), custom_call_target="tpu_custom_call" | custom-call | tf_op jit(solution)/shard_map/attend/attend_group/pallas_call | solution.py:283
  160.1 127.9 %all_to_all.10 = bf16[256,8,1280]{2,1,0:T(8,128)(2,1)} all-to-all(bf16[256,8,1280]{2,1,0:T(8,128)(2,1)} %bitcast.8), channel_id=1, replica_groups=mesh['grp'=32,'sp'=8] {'sp','grp'}, dimensions={0} | all-to-all | bytes 10485760 | tf_op jit(solution)/shard_map/to_homes/all_to_all | solution.py:313
  288.0 4.9 %unpack_rows.1 = (bf16[128,4096]{1,0:T(8,128)(2,1)}, bf16[128,4096]{1,0:T(8,128)(2,1)}, bf16[128,1024]{1,0:T(8,128)(2,1)}, bf16[128,1024]{1,0:T(8,128)(2,1)}) custom-call(s32[1,128]{1,0:T(1,128)} %refs_0_.3, bf16[8,256,1280]{2,1,0:T(8,128)(2,1)} %bitcast.7), custom_call_target="tpu_custom_call" | custom-call | tf_op jit(solution)/shard_map/unpack/unpack_rows/pallas_call | solution.py:260
Async XLA Ops:
  6.3 15.3 %copy-start = (s32[1,128]{1,0:T(1,128)S(1)}, s32[1,128]{1,0:T(1,128)}, u32[]{:S(2)}) copy-start(s32[1,128]{1,0:T(1,128)} %param.12) | copy-start | bytes 1540
  6.3 134.6 %all-to-all-start = ((bf16[256,8,1280]{2,1,0:T(8,128)(2,1)}), bf16[256,8,1280]{2,1,0:T(8,128)(2,1)}, u32[]{:S(2)}, u32[]{:S(2)}) async-start(bf16[256,8,1280]{2,1,0:T(8,128)(2,1)} %bitcast.6), calls=%async_computation | async-start | bytes 10485760 | tf_op jit(solution)/shard_map/to_groups/all_to_all | solution.py:313

commit v3 on v2

--- a/solution.py
+++ b/solution.py
@@ -10,7 +10,8 @@
 HEAD = 128
 F32 = jnp.float32
 BF16 = jnp.bfloat16
-VMEM_BYTES = 56 * 1024 * 1024
+VMEM_BYTES = 28 * 1024 * 1024
+PACK_VMEM_BYTES = 56 * 1024 * 1024
 
 
 def slot_tables(labels, capacity):
@@ -79,14 +80,11 @@
 
 
 def unpack_kernel(
-    capacity, labels_ref, got_hbm, o_hbm, dq_hbm, dk_hbm, dv_hbm, got_ref, o_ref, dq_ref, dk_ref, dv_ref, in_sem, out_sem
+    capacity, labels_ref, got_ref, o_hbm, dq_hbm, dk_hbm, dv_hbm, o_ref, dq_ref, dk_ref, dv_ref, out_sem
 ):
     columns, total, _ = got_ref.shape
     wide = o_ref.shape[1] // columns
     narrow = dk_ref.shape[1] // columns
-
-    def arrive(c):
-        return pltpu.make_async_copy(got_hbm.at[c], got_ref.at[c], in_sem.at[c])
 
     def column(c):
         pairs = ((o_ref, o_hbm, wide), (dq_ref, dq_hbm, wide), (dk_ref, dk_hbm, narrow), (dv_ref, dv_hbm, narrow))
@@ -97,12 +95,9 @@
             for n, (src, dst, size) in enumerate(pairs)
         ]
 
-    for c in range(columns):
-        arrive(c).start()
     _, slot_col = slot_tables(labels_ref[...], capacity)
     marks = one_hot_cols(slot_col, total)
     for c in range(columns):
-        arrive(c).wait()
         w = slice(c * wide, (c + 1) * wide)
         n = slice(c * narrow, (c + 1) * narrow)
         o_ref[:, w] = pick(marks, got_ref[c, :, :wide])
@@ -118,8 +113,8 @@
 
 
 def attend_kernel(
-    capacity, source_ref, start_ref, got_hbm, out_hbm, got_ref, out_ref, x_ref, s_ref, p_ref, pg_ref, w_ref, ds_ref,
-    kt_ref, vt_ref, dk_ref, dv_ref, in_sem, out_sem, last_sem,
+    capacity, source_ref, start_ref, got_ref, out_ref, x_ref, s_ref, p_ref, pg_ref, w_ref, ds_ref,
+    kt_ref, vt_ref, dk_ref, dv_ref,
 ):
     columns, total, width = got_ref.shape
     tok = source_ref.shape[1]
@@ -133,29 +128,15 @@
     joint = 2
     lanes = joint * tok
 
-    def arrive(s):
-        return pltpu.make_async_copy(got_hbm.at[s], got_ref.at[s], in_sem.at[s])
-
-    def leave(s):
-        cols = pl.ds(0, 2 * wide)
-        return pltpu.make_async_copy(out_ref.at[s, :, cols], out_hbm.at[s, :, cols], out_sem.at[s])
-
-    def leave_last(s):
-        cols = pl.ds(2 * wide, 2 * HEAD)
-        return pltpu.make_async_copy(out_ref.at[s, :, cols], out_hbm.at[s, :, cols], last_sem.at[s])
-
     def fold(values, op):
         return op(values.reshape(tok // 8, 8, lanes), axis=0)
 
-    for s in range(columns):
-        arrive(s).start()
     slots = [slot_tables(source_ref[s : s + 1, :], capacity) for s in range(columns)]
     place = lax.broadcasted_iota(jnp.int32, (tok, lanes), 0)
     lane = lax.broadcasted_iota(jnp.int32, (tok, lanes), 1) % tok
     for s in range(columns):
         rows = slice(s * tok, (s + 1) * tok)
         seen = (s + 1) * tok
-        arrive(s).wait()
         x_ref[rows, :] = pick(one_hot_cols(slots[s][1], total), got_ref[s])
         kt_ref[:, rows] = x_ref[rows, k_cols].astype(F32).T.astype(BF16)
         vt_ref[:, rows] = x_ref[rows, v_cols].astype(F32).T.astype(BF16)
@@ -210,7 +191,6 @@
             out_ref[s, :, base : base + wide] = lax.dot_general(
                 marks, stacked, across, preferred_element_type=F32
             ).astype(BF16)
-        leave(s).start()
         for total_ref, pairs, others in ((dk_ref, dscore, q), (dv_ref, weights, g)):
             result = jnp.dot(pairs, others, preferred_element_type=F32)
             if s:
@@ -220,14 +200,10 @@
         rows = slice(s * tok, (s + 1) * tok)
         last = jnp.concatenate([dk_ref[rows, :], dv_ref[rows, :]], axis=1).astype(BF16)
         out_ref[s, :, 2 * wide :] = pick(one_hot_rows(slots[s][0], total), last)
-        leave_last(s).start()
-    for s in range(columns):
-        leave(s).wait()
-        leave_last(s).wait()
-
-
-def params():
-    return pltpu.CompilerParams(vmem_limit_bytes=VMEM_BYTES)
+
+
+def params(limit=VMEM_BYTES):
+    return pltpu.CompilerParams(vmem_limit_bytes=limit)
 
 
 def pack(labels, queries, grads, keys, values, columns, total, capacity):
@@ -247,7 +223,7 @@
             pltpu.SemaphoreType.DMA((4, columns)),
             pltpu.SemaphoreType.DMA((columns,)),
         ],
-        compiler_params=params(),
+        compiler_params=params(PACK_VMEM_BYTES),
         name="pack_rows",
     )(labels, queries, grads, keys, values)
 
@@ -256,16 +232,15 @@
     columns, _, _ = got.shape
     tok = labels.shape[1]
     far = pl.BlockSpec(memory_space=pl.ANY)
+    near = pl.BlockSpec(memory_space=pltpu.VMEM)
     shapes = [(tok, columns * size) for size in (wide, wide, HEAD, HEAD)]
     return pl.pallas_call(
         lambda *refs: unpack_kernel(capacity, *refs),
-        in_specs=[pl.BlockSpec(memory_space=pltpu.VMEM), far],
+        in_specs=[near, near],
         out_specs=[far] * 4,
         out_shape=[jax.ShapeDtypeStruct(shape, BF16) for shape in shapes],
         scratch_shapes=[
-            pltpu.VMEM(got.shape, BF16),
             *[pltpu.VMEM(shape, BF16) for shape in shapes],
-            pltpu.SemaphoreType.DMA((columns,)),
             pltpu.SemaphoreType.DMA((4, columns)),
         ],
         compiler_params=params(),
@@ -279,15 +254,12 @@
     rows = starts.shape[1]
     pairs = (width - 2 * HEAD) // (2 * HEAD) * tok
     near = pl.BlockSpec(memory_space=pltpu.VMEM)
-    far = pl.BlockSpec(memory_space=pl.ANY)
     return pl.pallas_call(
         lambda *refs: attend_kernel(capacity, *refs),
-        in_specs=[near, near, far],
-        out_specs=far,
-        out_shape=jax.ShapeDtypeStruct(got.shape, BF16),
+        in_specs=[near, near, near],
+        out_specs=near,
+        out_shape=pltpu.VMEM(got.shape, BF16),
         scratch_shapes=[
-            pltpu.VMEM(got.shape, BF16),
-            pltpu.VMEM(got.shape, BF16),
             pltpu.VMEM((rows, width), BF16),
             pltpu.VMEM((rows, 2 * tok), F32),
             pltpu.VMEM((rows, 2 * tok), F32),
@@ -298,9 +270,6 @@
             pltpu.VMEM((HEAD, rows), BF16),
             pltpu.VMEM((rows, HEAD), F32),
             pltpu.VMEM((rows, HEAD), F32),
-            pltpu.SemaphoreType.DMA((columns,)),
-            pltpu.SemaphoreType.DMA((columns,)),
-            pltpu.SemaphoreType.DMA((columns,)),
         ],
         compiler_params=params(),
         name="attend_group",
@@ -311,7 +280,8 @@
     _, total, width = rows.shape
     blocks = rows.reshape(columns * groups, total // groups, width)
     moved = lax.all_to_all(blocks, ("sp", "grp"), split_axis=0, concat_axis=0, tiled=True)
-    return moved.reshape(columns, total, width)
+    moved = moved.reshape(columns, total, width)
+    return pltpu.with_memory_space_constraint(moved, pltpu.VMEM)
 
 
 def per_device(

time: 294 us -> 288 us (0.980)
  Pallas kernels: 29.7 us -> 25 us
where the time goes in v3:
time: 288 us; the launch traced here: 287 us
  blocking collectives  143 us (50%)
  waiting for transfers between devices  103 us (36%)
  Pallas kernels  25 us (9%)
  starting transfers between devices  15.3 us (5%)
    all_to_all x1, blocking collectives, swap(): lax.all_to_all(blocks, ('sp', 'grp'), split_axis=0, concat_axis=0, tiled=...  127 us
    all_to_all x1, waiting for transfers between devices, swap(): lax.all_to_all(blocks, ('sp', 'grp'), split_axis=0, concat_axis=0, tiled=...  103 us
    pallas_call x1, Pallas kernels, attend(): pl.pallas_call(lambda *refs: attend_kernel(capacity, *refs), in_specs=[ne...  17.2 us
    all_gather x1, blocking collectives, per_device(): sources = lax.all_gather(source_group, 'sp', axis=0, tiled=True)  16.1 us
    all_to_all x1, starting transfers between devices, swap(): lax.all_to_all(blocks, ('sp', 'grp'), split_axis=0, concat_axis=0, tiled=...  15.3 us
  transfers between devices with their start and end apart: 1, of which 1 were waited for; matrix products, arithmetic and copies ran while one was open for 0% of the time, Pallas kernels for 0%

profile of v3, /device:TPU:32, one launch (start us, length us, event | category | flops | bytes accessed | tf_op | source)
XLA Modules:
  0.0 287.1 jit_solution(16903559627837429565)
XLA Ops:
  0.6 5.7 %pack_rows.1 = bf16[8,256,1280]{2,1,0:T(8,128)(2,1)} custom-call(s32[1,128]{1,0:T(1,128)} %refs_0_.3, bf16[128,4096]{1,0:T(8,128)(2,1)} %refs_1_.2, bf16[128,4096]{1,0:T(8,128)(2,1)} %refs_2_.1, bf16[128,1024]{1,0:T(8,128)(2,1)} %refs_3_.1, bf16[128,1024]{1,0:T(8,128)(2,1)} %refs_4_.1), custom_call_target="tpu_custom_call" | custom-call | tf_op jit(solution)/shard_map/pack/pack_rows/pallas_call | solution.py:212
  6.3 0.0 copy-start.2
  6.3 0.0 copy-start
  6.3 15.3 %all-to-all-start = ((bf16[256,8,1280]{2,1,0:T(8,128)(2,1)}), bf16[256,8,1280]{2,1,0:T(8,128)(2,1)}, u32[]{:S(2)}, u32[]{:S(2)}) async-start(bf16[256,8,1280]{2,1,0:T(8,128)(2,1)} %bitcast.9), calls=%async_computation | async-start | bytes 10485760 | tf_op jit(solution)/shard_map/to_groups/all_to_all | solution.py:282
  21.6 0.0 copy-done.2
  21.6 16.1 %all-gather = s32[8,1,128]{2,1,0:T(1,128)S(1)} all-gather(s32[1,1,128]{2,1,0:T(1,128)S(1)} %bitcast.10), channel_id=1, replica_groups=mesh['grp'=32,'sp'=8] {'sp'}, dimensions={0}, use_global_device_ids=true | all-gather | bytes 4608 | tf_op jit(solution)/shard_map/tables/all_gather | solution.py:301
  37.7 103.2 %all-to-all-done = bf16[256,8,1280]{2,1,0:T(8,128)(2,1)} async-done(((bf16[256,8,1280]{2,1,0:T(8,128)(2,1)}), bf16[256,8,1280]{2,1,0:T(8,128)(2,1)}, u32[]{:S(2)}, u32[]{:S(2)}) %all-to-all-start) | async-done | bytes 5242912 | tf_op jit(solution)/shard_map/to_groups/all_to_all | solution.py:282
  140.9 0.0 copy-done
  140.9 17.2 %attend_group.1 = bf16[8,256,1280]{2,1,0:T(8,128)(2,1)S(1)} custom-call(s32[8,128]{1,0:T(8,128)S(1)} %bitcast.8, s32[1,1024]{1,0:T(1,128)S(1)} %copy-done, bf16[8,256,1280]{2,1,0:T(8,128)(2,1)} %bitcast.3.refs_2_), custom_call_target="tpu_custom_call" | custom-call | tf_op jit(solution)/shard_map/attend/attend_group/pallas_call | solution.py:257
  158.1 0.0 copy-start.1
  158.1 126.7 %all_to_all.10 = bf16[256,8,1280]{2,1,0:T(8,128)(2,1)S(1)} all-to-all(bf16[256,8,1280]{2,1,0:T(8,128)(2,1)S(1)} %bitcast.7), channel_id=1, replica_groups=mesh['grp'=32,'sp'=8] {'sp','grp'}, dimensions={0} | all-to-all | bytes 10485760 | tf_op jit(solution)/shard_map/to_homes/all_to_all | solution.py:282
  284.8 0.0 copy-done.1
  284.8 2.1 unpack_rows.1
Async XLA Ops:
  6.3 15.3 %copy-start.2 = (s32[1,128]{1,0:T(1,128)S(1)}, s32[1,128]{1,0:T(1,128)}, u32[]{:S(2)}) copy-start(s32[1,128]{1,0:T(1,128)} %param.12) | copy-start | bytes 1540
  6.3 134.6 %copy-start = (s32[1,1024]{1,0:T(1,128)S(1)}, s32[1,1024]{1,0:T(1,128)}, u32[]{:S(2)}) copy-start(s32[1,1024]{1,0:T(1,128)} %refs_1_.3) | copy-start | bytes 12292
  6.3 134.6 %all-to-all-start = ((bf16[256,8,1280]{2,1,0:T(8,128)(2,1)}), bf16[256,8,1280]{2,1,0:T(8,128)(2,1)}, u32[]{:S(2)}, u32[]{:S(2)}) async-start(bf16[256,8,1280]{2,1,0:T(8,128)(2,1)} %bitcast.9), calls=%async_computation | async-start | bytes 10485760 | tf_op jit(solution)/shard_map/to_groups/all_to_all | solution.py:282
  158.1 126.7 %copy-start.1 = (s32[1,128]{1,0:T(1,128)S(1)}, s32[1,128]{1,0:T(1,128)}, u32[]{:S(2)}) copy-start(s32[1,128]{1,0:T(1,128)} %refs_0_.3) | copy-start | bytes 1540

commit v4 on v3

--- a/solution.py
+++ b/solution.py
@@ -10,8 +10,8 @@
 HEAD = 128
 F32 = jnp.float32
 BF16 = jnp.bfloat16
-VMEM_BYTES = 28 * 1024 * 1024
-PACK_VMEM_BYTES = 56 * 1024 * 1024
+VMEM_BYTES = 56 * 1024 * 1024
+UNPACK_VMEM_BYTES = 28 * 1024 * 1024
 
 
 def slot_tables(labels, capacity):
@@ -49,11 +49,16 @@
     wide = q_ref.shape[1] // columns
     narrow = k_ref.shape[1] // columns
 
+    parts = 2
+    span = columns // parts
+
     def column(c):
         pairs = ((q_hbm, q_ref, wide), (g_hbm, g_ref, wide), (k_hbm, k_ref, narrow), (v_hbm, v_ref, narrow))
         return [
             pltpu.make_async_copy(
-                src.at[:, pl.ds(c * size, size)], dst.at[:, pl.ds(c * size, size)], in_sem.at[n, c]
+                src.at[:, pl.ds(c * span * size, span * size)],
+                dst.at[:, pl.ds(c * span * size, span * size)],
+                in_sem.at[n, c],
             )
             for n, (src, dst, size) in enumerate(pairs)
         ]
@@ -61,14 +66,15 @@
     def leave(c):
         return pltpu.make_async_copy(out_ref.at[c], out_hbm.at[c], out_sem.at[c])
 
-    for c in range(columns):
+    for c in range(parts):
         for copy in column(c):
             copy.start()
     slot_row, _ = slot_tables(labels_ref[...], capacity)
     marks = one_hot_rows(slot_row, total)
     for c in range(columns):
-        for copy in column(c):
-            copy.wait()
+        if c % span == 0:
+            for copy in column(c // span):
+                copy.wait()
         w = slice(c * wide, (c + 1) * wide)
         n = slice(c * narrow, (c + 1) * narrow)
         out_ref[c, :, :wide] = pick(marks, q_ref[:, w])
@@ -113,8 +119,8 @@
 
 
 def attend_kernel(
-    capacity, source_ref, start_ref, got_ref, out_ref, x_ref, s_ref, p_ref, pg_ref, w_ref, ds_ref,
-    kt_ref, vt_ref, dk_ref, dv_ref,
+    capacity, source_ref, start_ref, got_hbm, out_ref, got_ref, x_ref, s_ref, p_ref, pg_ref, w_ref, ds_ref,
+    kt_ref, vt_ref, dk_ref, dv_ref, in_sem,
 ):
     columns, total, width = got_ref.shape
     tok = source_ref.shape[1]
@@ -128,76 +134,132 @@
     joint = 2
     lanes = joint * tok
 
+    def arrive(s):
+        return pltpu.make_async_copy(got_hbm.at[s], got_ref.at[s], in_sem.at[s])
+
     def fold(values, op):
         return op(values.reshape(tok // 8, 8, lanes), axis=0)
 
+    for s in range(columns):
+        arrive(s).start()
     slots = [slot_tables(source_ref[s : s + 1, :], capacity) for s in range(columns)]
     place = lax.broadcasted_iota(jnp.int32, (tok, lanes), 0)
     lane = lax.broadcasted_iota(jnp.int32, (tok, lanes), 1) % tok
-    for s in range(columns):
-        rows = slice(s * tok, (s + 1) * tok)
-        seen = (s + 1) * tok
+
+    def block(s):
+        return slice(s * tok, (s + 1) * tok)
+
+    def stack(s, base, heads):
+        return jnp.concatenate(
+            [x_ref[block(s), base + h * HEAD : base + (h + 1) * HEAD] for h in heads], axis=0
+        )
+
+    def receive(s):
+        rows = block(s)
+        if s == 0:
+            arrive(0).wait()
+        elif s == 1:
+            for n in range(1, columns):
+                arrive(n).wait()
         x_ref[rows, :] = pick(one_hot_cols(slots[s][1], total), got_ref[s])
         kt_ref[:, rows] = x_ref[rows, k_cols].astype(F32).T.astype(BF16)
         vt_ref[:, rows] = x_ref[rows, v_cols].astype(F32).T.astype(BF16)
-        start = jnp.concatenate([start_ref[:, rows]] * joint, axis=1)
-        for first in range(0, share, joint):
-            heads = range(first, first + joint)
-            part = slice(first * tok, first * tok + lanes)
-            q = jnp.concatenate([x_ref[rows, h * HEAD : (h + 1) * HEAD] for h in heads], axis=0)
-            g = jnp.concatenate(
-                [x_ref[rows, wide + h * HEAD : wide + (h + 1) * HEAD] for h in heads], axis=0
-            )
+
+    def softmax_steps(s, first):
+        heads = range(first, first + joint)
+        part = slice(first * tok, first * tok + lanes)
+        side = (first // joint) % 2
+        turn = s % 2
+        state = {}
+
+        def score():
+            q = stack(s, 0, heads)
+            start = jnp.concatenate([start_ref[:, block(s)]] * joint, axis=1)
             top = None
             for t in range(s + 1):
-                keys = slice(t * tok, (t + 1) * tok)
+                keys = block(t)
                 scores = lax.dot_general(x_ref[keys, k_cols], q, across, preferred_element_type=F32)
                 visible = place >= start - t * tok
                 if t == s:
                     visible = visible & (place <= lane)
                 scores = jnp.where(visible, scores, -jnp.inf)
-                s_ref[keys, :] = scores
+                s_ref[side, keys, :] = scores
                 best = fold(scores, jnp.max)
                 top = best if top is None else jnp.maximum(top, best)
-            top = jnp.max(top, axis=0, keepdims=True)
+            state["top"] = jnp.max(top, axis=0, keepdims=True)
+
+        def power():
+            g = stack(s, wide, heads)
             mass = jnp.zeros((8, lanes), F32)
             spread = jnp.zeros((8, lanes), F32)
             for t in range(s + 1):
-                keys = slice(t * tok, (t + 1) * tok)
-                powers = jnp.exp2((s_ref[keys, :] - top) * power_scale)
+                keys = block(t)
+                powers = jnp.exp2((s_ref[side, keys, :] - state["top"]) * power_scale)
                 prob_grad = lax.dot_general(x_ref[keys, v_cols], g, across, preferred_element_type=F32)
-                p_ref[keys, :] = powers
-                pg_ref[keys, :] = prob_grad
+                p_ref[side, keys, :] = powers
+                pg_ref[side, keys, :] = prob_grad
                 mass = mass + fold(powers, jnp.sum)
                 spread = spread + fold(powers * prob_grad, jnp.sum)
-            inverse = 1.0 / jnp.sum(mass, axis=0, keepdims=True)
-            spread = jnp.sum(spread, axis=0, keepdims=True) * inverse
+            state["inverse"] = 1.0 / jnp.sum(mass, axis=0, keepdims=True)
+            state["spread"] = jnp.sum(spread, axis=0, keepdims=True) * state["inverse"]
+
+        def finish():
+            inverse, spread = state["inverse"], state["spread"]
             scaled = inverse * scaling
             for t in range(s + 1):
-                keys = slice(t * tok, (t + 1) * tok)
-                powers = p_ref[keys, :]
-                w_ref[keys, part] = (powers * inverse).astype(BF16)
-                ds_ref[keys, part] = ((powers * scaled) * (pg_ref[keys, :] - spread)).astype(BF16)
-        weights = w_ref[:seen, :]
-        dscore = ds_ref[:seen, :]
-        q = jnp.concatenate([x_ref[rows, h * HEAD : (h + 1) * HEAD] for h in range(share)], axis=0)
-        g = jnp.concatenate(
-            [x_ref[rows, wide + h * HEAD : wide + (h + 1) * HEAD] for h in range(share)], axis=0
-        )
-        marks = one_hot_rows(slots[s][0], total)
-        for base, turned, pairs in ((0, vt_ref, weights), (wide, kt_ref, dscore)):
-            result = jnp.dot(turned[:, :seen], pairs, preferred_element_type=F32).astype(BF16)
+                keys = block(t)
+                powers = p_ref[side, keys, :]
+                w_ref[turn, keys, part] = (powers * inverse).astype(BF16)
+                ds_ref[turn, keys, part] = ((powers * scaled) * (pg_ref[side, keys, :] - spread)).astype(BF16)
+
+        return [score, power, finish]
+
+    def product_steps(s):
+        seen = (s + 1) * tok
+        rows = block(s)
+        turn = s % 2
+
+        def rowwise(base, turned, pairs_ref):
+            marks = one_hot_rows(slots[s][0], total)
+            result = jnp.dot(turned[:, :seen], pairs_ref[turn, :seen, :], preferred_element_type=F32)
+            result = result.astype(BF16)
             stacked = jnp.concatenate([result[:, h * tok : (h + 1) * tok] for h in range(share)], axis=0)
             out_ref[s, :, base : base + wide] = lax.dot_general(
                 marks, stacked, across, preferred_element_type=F32
             ).astype(BF16)
-        for total_ref, pairs, others in ((dk_ref, dscore, q), (dv_ref, weights, g)):
-            result = jnp.dot(pairs, others, preferred_element_type=F32)
+
+        def keywise(total_ref, pairs_ref, base):
+            others = stack(s, base, range(share))
+            result = jnp.dot(pairs_ref[turn, :seen, :], others, preferred_element_type=F32)
             if s:
                 total_ref[: s * tok, :] += result[: s * tok]
             total_ref[rows, :] = result[s * tok :]
+
+        return [
+            lambda: rowwise(0, vt_ref, w_ref),
+            lambda: keywise(dv_ref, w_ref, wide),
+            lambda: rowwise(wide, kt_ref, ds_ref),
+            lambda: keywise(dk_ref, ds_ref, 0),
+        ]
+
+    receive(0)
+    waiting = []
     for s in range(columns):
-        rows = slice(s * tok, (s + 1) * tok)
+        lists = [softmax_steps(s, first) for first in range(0, share, joint)]
+        work = [step for group in zip(*lists) for step in group]
+        if s + 1 < columns:
+            waiting = waiting + [lambda n=s + 1: receive(n)]
+        for n, step in enumerate(work):
+            step()
+            if n < len(waiting):
+                waiting[n]()
+        for step in waiting[len(work) :]:
+            step()
+        waiting = product_steps(s)
+    for step in waiting:
+        step()
+    for s in range(columns):
+        rows = block(s)
         last = jnp.concatenate([dk_ref[rows, :], dv_ref[rows, :]], axis=1).astype(BF16)
         out_ref[s, :, 2 * wide :] = pick(one_hot_rows(slots[s][0], total), last)
 
@@ -223,7 +285,7 @@
             pltpu.SemaphoreType.DMA((4, columns)),
             pltpu.SemaphoreType.DMA((columns,)),
         ],
-        compiler_params=params(PACK_VMEM_BYTES),
+        compiler_params=params(),
         name="pack_rows",
     )(labels, queries, grads, keys, values)
 
@@ -243,7 +305,7 @@
             *[pltpu.VMEM(shape, BF16) for shape in shapes],
             pltpu.SemaphoreType.DMA((4, columns)),
         ],
-        compiler_params=params(),
+        compiler_params=params(UNPACK_VMEM_BYTES),
         name="unpack_rows",
     )(labels, got)
 
@@ -256,20 +318,22 @@
     near = pl.BlockSpec(memory_space=pltpu.VMEM)
     return pl.pallas_call(
         lambda *refs: attend_kernel(capacity, *refs),
-        in_specs=[near, near, near],
+        in_specs=[near, near, pl.BlockSpec(memory_space=pl.ANY)],
         out_specs=near,
         out_shape=pltpu.VMEM(got.shape, BF16),
         scratch_shapes=[
+            pltpu.VMEM(got.shape, BF16),
             pltpu.VMEM((rows, width), BF16),
-            pltpu.VMEM((rows, 2 * tok), F32),
-            pltpu.VMEM((rows, 2 * tok), F32),
-            pltpu.VMEM((rows, 2 * tok), F32),
-            pltpu.VMEM((rows, pairs), BF16),
-            pltpu.VMEM((rows, pairs), BF16),
+            pltpu.VMEM((2, rows, 2 * tok), F32),
+            pltpu.VMEM((2, rows, 2 * tok), F32),
+            pltpu.VMEM((2, rows, 2 * tok), F32),
+            pltpu.VMEM((2, rows, pairs), BF16),
+            pltpu.VMEM((2, rows, pairs), BF16),
             pltpu.VMEM((HEAD, rows), BF16),
             pltpu.VMEM((HEAD, rows), BF16),
             pltpu.VMEM((rows, HEAD), F32),
             pltpu.VMEM((rows, HEAD), F32),
+            pltpu.SemaphoreType.DMA((columns,)),
         ],
         compiler_params=params(),
         name="attend_group",
@@ -280,8 +344,7 @@
     _, total, width = rows.shape
     blocks = rows.reshape(columns * groups, total // groups, width)
     moved = lax.all_to_all(blocks, ("sp", "grp"), split_axis=0, concat_axis=0, tiled=True)
-    moved = moved.reshape(columns, total, width)
-    return pltpu.with_memory_space_constraint(moved, pltpu.VMEM)
+    return moved.reshape(columns, total, width)
 
 
 def per_device(
@@ -304,7 +367,7 @@
     with jax.named_scope("attend"):
         done = attend(got, sources, seq_start, capacity)
     with jax.named_scope("to_homes"):
-        back = swap(done, columns, groups)
+        back = pltpu.with_memory_space_constraint(swap(done, columns, groups), pltpu.VMEM)
     with jax.named_scope("unpack"):
         return tuple(unpack(dest_group, back, wide, capacity))
 

time: 288 us -> 286 us (level)
  no operation moved by 1% of the time
where the time goes in v4:
time: 286 us; the launch traced here: 285 us
  blocking collectives  143 us (50%)
  waiting for transfers between devices  103 us (36%)
  Pallas kernels  23 us (8%)
  starting transfers between devices  15.3 us (5%)
    all_to_all x1, blocking collectives, swap(): lax.all_to_all(blocks, ('sp', 'grp'), split_axis=0, concat_axis=0, tiled=...  127 us
    all_to_all x1, waiting for transfers between devices, swap(): lax.all_to_all(blocks, ('sp', 'grp'), split_axis=0, concat_axis=0, tiled=...  103 us
    all_gather x1, blocking collectives, per_device(): sources = lax.all_gather(source_group, 'sp', axis=0, tiled=True)  16.3 us
    pallas_call x1, Pallas kernels, attend(): pl.pallas_call(lambda *refs: attend_kernel(capacity, *refs), in_specs=[ne...  15.9 us
    all_to_all x1, starting transfers between devices, swap(): lax.all_to_all(blocks, ('sp', 'grp'), split_axis=0, concat_axis=0, tiled=...  15.3 us
  transfers between devices with their start and end apart: 1, of which 1 were waited for; matrix products, arithmetic and copies ran while one was open for 0% of the time, Pallas kernels for 0%

profile of v4, /device:TPU:32, one launch (start us, length us, event | category | flops | bytes accessed | tf_op | source)
XLA Modules:
  0.0 285.2 jit_solution(11421998642724536679)
XLA Ops:
  0.6 5.0 %pack_rows.1 = bf16[8,256,1280]{2,1,0:T(8,128)(2,1)} custom-call(s32[1,128]{1,0:T(1,128)} %refs_0_.3, bf16[128,4096]{1,0:T(8,128)(2,1)} %refs_1_.2, bf16[128,4096]{1,0:T(8,128)(2,1)} %refs_2_.1, bf16[128,1024]{1,0:T(8,128)(2,1)} %refs_3_.1, bf16[128,1024]{1,0:T(8,128)(2,1)} %refs_4_.1), custom_call_target="tpu_custom_call" | custom-call | tf_op jit(solution)/shard_map/pack/pack_rows/pallas_call | solution.py:274
  5.6 0.0 copy-start.1
  5.7 15.3 %all-to-all-start = ((bf16[256,8,1280]{2,1,0:T(8,128)(2,1)}), bf16[256,8,1280]{2,1,0:T(8,128)(2,1)}, u32[]{:S(2)}, u32[]{:S(2)}) async-start(bf16[256,8,1280]{2,1,0:T(8,128)(2,1)} %bitcast.8), calls=%async_computation | async-start | bytes 10485760 | tf_op jit(solution)/shard_map/to_groups/all_to_all | solution.py:346
  20.9 0.0 copy-done.1
  20.9 16.3 %all-gather = s32[8,1,128]{2,1,0:T(1,128)} all-gather(s32[1,1,128]{2,1,0:T(1,128)S(1)} %bitcast.10), channel_id=1, replica_groups=mesh['grp'=32,'sp'=8] {'sp'}, dimensions={0}, use_global_device_ids=true | all-gather | bytes 4608 | tf_op jit(solution)/shard_map/tables/all_gather | solution.py:364
  37.2 103.0 %all-to-all-done = bf16[256,8,1280]{2,1,0:T(8,128)(2,1)} async-done(((bf16[256,8,1280]{2,1,0:T(8,128)(2,1)}), bf16[256,8,1280]{2,1,0:T(8,128)(2,1)}, u32[]{:S(2)}, u32[]{:S(2)}) %all-to-all-start) | async-done | bytes 5242912 | tf_op jit(solution)/shard_map/to_groups/all_to_all | solution.py:346
  140.2 15.9 %attend_group.1 = bf16[8,256,1280]{2,1,0:T(8,128)(2,1)S(1)} custom-call(s32[8,128]{1,0:T(8,128)} %bitcast.9, s32[1,1024]{1,0:T(1,128)} %refs_1_.3, bf16[8,256,1280]{2,1,0:T(8,128)(2,1)} %bitcast.3.refs_2_), custom_call_target="tpu_custom_call" | custom-call | tf_op jit(solution)/shard_map/attend/attend_group/pallas_call | solution.py:319
  156.1 0.0 copy-start
  156.1 126.7 %all_to_all.10 = bf16[256,8,1280]{2,1,0:T(8,128)(2,1)S(1)} all-to-all(bf16[256,8,1280]{2,1,0:T(8,128)(2,1)S(1)} %bitcast.7), channel_id=1, replica_groups=mesh['grp'=32,'sp'=8] {'sp','grp'}, dimensions={0} | all-to-all | bytes 10485760 | tf_op jit(solution)/shard_map/to_homes/all_to_all | solution.py:346
  282.8 0.0 copy-done
  282.8 2.1 unpack_rows.1
Async XLA Ops:
  5.6 15.3 %copy-start.1 = (s32[1,128]{1,0:T(1,128)S(1)}, s32[1,128]{1,0:T(1,128)}, u32[]{:S(2)}) copy-start(s32[1,128]{1,0:T(1,128)} %param.12) | copy-start | bytes 1540
  5.7 134.6 %all-to-all-start = ((bf16[256,8,1280]{2,1,0:T(8,128)(2,1)}), bf16[256,8,1280]{2,1,0:T(8,128)(2,1)}, u32[]{:S(2)}, u32[]{:S(2)}) async-start(bf16[256,8,1280]{2,1,0:T(8,128)(2,1)} %bitcast.8), calls=%async_computation | async-start | bytes 10485760 | tf_op jit(solution)/shard_map/to_groups/all_to_all | solution.py:346
  156.1 126.7 %copy-start = (s32[1,128]{1,0:T(1,128)S(1)}, s32[1,128]{1,0:T(1,128)}, u32[]{:S(2)}) copy-start(s32[1,128]{1,0:T(1,128)} %refs_0_.3) | copy-start | bytes 1540

commit v5 on v4

--- a/solution.py
+++ b/solution.py
@@ -10,6 +10,7 @@
 HEAD = 128
 F32 = jnp.float32
 BF16 = jnp.bfloat16
+CHUNK = 8
 VMEM_BYTES = 56 * 1024 * 1024
 UNPACK_VMEM_BYTES = 28 * 1024 * 1024
 
@@ -138,13 +139,16 @@
         return pltpu.make_async_copy(got_hbm.at[s], got_ref.at[s], in_sem.at[s])
 
     def fold(values, op):
-        return op(values.reshape(tok // 8, 8, lanes), axis=0)
+        return op(values.reshape(values.shape[0] // 8, 8, lanes), axis=0)
+
+    def spans(s):
+        return [(t, min(t + CHUNK, s + 1)) for t in range(0, s + 1, CHUNK)]
 
     for s in range(columns):
         arrive(s).start()
     slots = [slot_tables(source_ref[s : s + 1, :], capacity) for s in range(columns)]
-    place = lax.broadcasted_iota(jnp.int32, (tok, lanes), 0)
-    lane = lax.broadcasted_iota(jnp.int32, (tok, lanes), 1) % tok
+    place = lax.broadcasted_iota(jnp.int32, (CHUNK * tok, lanes), 0)
+    lane = lax.broadcasted_iota(jnp.int32, (CHUNK * tok, lanes), 1) % tok
 
     def block(s):
         return slice(s * tok, (s + 1) * tok)
@@ -156,11 +160,8 @@
 
     def receive(s):
         rows = block(s)
-        if s == 0:
-            arrive(0).wait()
-        elif s == 1:
-            for n in range(1, columns):
-                arrive(n).wait()
+        for n in {0: range(2), 2: range(2, columns)}.get(s, ()):
+            arrive(n).wait()
         x_ref[rows, :] = pick(one_hot_cols(slots[s][1], total), got_ref[s])
         kt_ref[:, rows] = x_ref[rows, k_cols].astype(F32).T.astype(BF16)
         vt_ref[:, rows] = x_ref[rows, v_cols].astype(F32).T.astype(BF16)
@@ -176,12 +177,13 @@
             q = stack(s, 0, heads)
             start = jnp.concatenate([start_ref[:, block(s)]] * joint, axis=1)
             top = None
-            for t in range(s + 1):
-                keys = block(t)
+            for t, end in spans(s):
+                keys = slice(t * tok, end * tok)
                 scores = lax.dot_general(x_ref[keys, k_cols], q, across, preferred_element_type=F32)
-                visible = place >= start - t * tok
-                if t == s:
-                    visible = visible & (place <= lane)
+                size = (end - t) * tok
+                visible = place[:size] >= start - t * tok
+                if end == s + 1:
+                    visible = visible & (place[:size] <= lane[:size] + (s - t) * tok)
                 scores = jnp.where(visible, scores, -jnp.inf)
                 s_ref[side, keys, :] = scores
                 best = fold(scores, jnp.max)
@@ -192,8 +194,8 @@
             g = stack(s, wide, heads)
             mass = jnp.zeros((8, lanes), F32)
             spread = jnp.zeros((8, lanes), F32)
-            for t in range(s + 1):
-                keys = block(t)
+            for t, end in spans(s):
+                keys = slice(t * tok, end * tok)
                 powers = jnp.exp2((s_ref[side, keys, :] - state["top"]) * power_scale)
                 prob_grad = lax.dot_general(x_ref[keys, v_cols], g, across, preferred_element_type=F32)
                 p_ref[side, keys, :] = powers
@@ -206,8 +208,8 @@
         def finish():
             inverse, spread = state["inverse"], state["spread"]
             scaled = inverse * scaling
-            for t in range(s + 1):
-                keys = block(t)
+            for t, end in spans(s):
+                keys = slice(t * tok, end * tok)
                 powers = p_ref[side, keys, :]
                 w_ref[turn, keys, part] = (powers * inverse).astype(BF16)
                 ds_ref[turn, keys, part] = ((powers * scaled) * (pg_ref[side, keys, :] - spread)).astype(BF16)

time: 286 us -> 285 us (level)
  no operation moved by 1% of the time
where the time goes in v5:
time: 285 us; the launch traced here: 284 us
  blocking collectives  143 us (50%)
  waiting for transfers between devices  103 us (36%)
  Pallas kernels  21.8 us (8%)
  starting transfers between devices  15.3 us (5%)
    all_to_all x1, blocking collectives, swap(): lax.all_to_all(blocks, ('sp', 'grp'), split_axis=0, concat_axis=0, tiled=...  127 us
    all_to_all x1, waiting for transfers between devices, swap(): lax.all_to_all(blocks, ('sp', 'grp'), split_axis=0, concat_axis=0, tiled=...  103 us
    all_gather x1, blocking collectives, per_device(): sources = lax.all_gather(source_group, 'sp', axis=0, tiled=True)  16.3 us
    all_to_all x1, starting transfers between devices, swap(): lax.all_to_all(blocks, ('sp', 'grp'), split_axis=0, concat_axis=0, tiled=...  15.3 us
    pallas_call x1, Pallas kernels, attend(): pl.pallas_call(lambda *refs: attend_kernel(capacity, *refs), in_specs=[ne...  14.7 us
  transfers between devices with their start and end apart: 1, of which 1 were waited for; matrix products, arithmetic and copies ran while one was open for 0% of the time, Pallas kernels for 0%

profile of v5, /device:TPU:32, one launch (start us, length us, event | category | flops | bytes accessed | tf_op | source)
XLA Modules:
  0.0 283.9 jit_solution(8508279222935309329)
XLA Ops:
  0.6 5.0 %pack_rows.1 = bf16[8,256,1280]{2,1,0:T(8,128)(2,1)} custom-call(s32[1,128]{1,0:T(1,128)} %refs_0_.3, bf16[128,4096]{1,0:T(8,128)(2,1)} %refs_1_.2, bf16[128,4096]{1,0:T(8,128)(2,1)} %refs_2_.1, bf16[128,1024]{1,0:T(8,128)(2,1)} %refs_3_.1, bf16[128,1024]{1,0:T(8,128)(2,1)} %refs_4_.1), custom_call_target="tpu_custom_call" | custom-call | tf_op jit(solution)/shard_map/pack/pack_rows/pallas_call | solution.py:276
  5.6 0.0 copy-start.1
  5.7 15.3 %all-to-all-start = ((bf16[256,8,1280]{2,1,0:T(8,128)(2,1)}), bf16[256,8,1280]{2,1,0:T(8,128)(2,1)}, u32[]{:S(2)}, u32[]{:S(2)}) async-start(bf16[256,8,1280]{2,1,0:T(8,128)(2,1)} %bitcast.8), calls=%async_computation | async-start | bytes 10485760 | tf_op jit(solution)/shard_map/to_groups/all_to_all | solution.py:348
  20.9 0.0 copy-done.1
  20.9 16.3 %all-gather = s32[8,1,128]{2,1,0:T(1,128)} all-gather(s32[1,1,128]{2,1,0:T(1,128)S(1)} %bitcast.10), channel_id=1, replica_groups=mesh['grp'=32,'sp'=8] {'sp'}, dimensions={0}, use_global_device_ids=true | all-gather | bytes 4608 | tf_op jit(solution)/shard_map/tables/all_gather | solution.py:366
  37.2 103.0 %all-to-all-done = bf16[256,8,1280]{2,1,0:T(8,128)(2,1)} async-done(((bf16[256,8,1280]{2,1,0:T(8,128)(2,1)}), bf16[256,8,1280]{2,1,0:T(8,128)(2,1)}, u32[]{:S(2)}, u32[]{:S(2)}) %all-to-all-start) | async-done | bytes 5242912 | tf_op jit(solution)/shard_map/to_groups/all_to_all | solution.py:348
  140.2 14.7 %attend_group.1 = bf16[8,256,1280]{2,1,0:T(8,128)(2,1)S(1)} custom-call(s32[8,128]{1,0:T(8,128)} %bitcast.9, s32[1,1024]{1,0:T(1,128)} %refs_1_.3, bf16[8,256,1280]{2,1,0:T(8,128)(2,1)} %bitcast.3.refs_2_), custom_call_target="tpu_custom_call" | custom-call | tf_op jit(solution)/shard_map/attend/attend_group/pallas_call | solution.py:321
  154.9 0.0 copy-start
  154.9 126.7 %all_to_all.10 = bf16[256,8,1280]{2,1,0:T(8,128)(2,1)S(1)} all-to-all(bf16[256,8,1280]{2,1,0:T(8,128)(2,1)S(1)} %bitcast.7), channel_id=1, replica_groups=mesh['grp'=32,'sp'=8] {'sp','grp'}, dimensions={0} | all-to-all | bytes 10485760 | tf_op jit(solution)/shard_map/to_homes/all_to_all | solution.py:348
  281.6 0.0 copy-done
  281.6 2.1 unpack_rows.1
Async XLA Ops:
  5.6 15.3 %copy-start.1 = (s32[1,128]{1,0:T(1,128)S(1)}, s32[1,128]{1,0:T(1,128)}, u32[]{:S(2)}) copy-start(s32[1,128]{1,0:T(1,128)} %param.12) | copy-start | bytes 1540
  5.7 134.6 %all-to-all-start = ((bf16[256,8,1280]{2,1,0:T(8,128)(2,1)}), bf16[256,8,1280]{2,1,0:T(8,128)(2,1)}, u32[]{:S(2)}, u32[]{:S(2)}) async-start(bf16[256,8,1280]{2,1,0:T(8,128)(2,1)} %bitcast.8), calls=%async_computation | async-start | bytes 10485760 | tf_op jit(solution)/shard_map/to_groups/all_to_all | solution.py:348
  154.9 126.7 %copy-start = (s32[1,128]{1,0:T(1,128)S(1)}, s32[1,128]{1,0:T(1,128)}, u32[]{:S(2)}) copy-start(s32[1,128]{1,0:T(1,128)} %refs_0_.3) | copy-start | bytes 1540

commit v6 on v5

--- a/solution.py
+++ b/solution.py
@@ -87,9 +87,9 @@
 
 
 def unpack_kernel(
-    capacity, labels_ref, got_ref, o_hbm, dq_hbm, dk_hbm, dv_hbm, o_ref, dq_ref, dk_ref, dv_ref, out_sem
+    marks_ref, got_ref, o_hbm, dq_hbm, dk_hbm, dv_hbm, o_ref, dq_ref, dk_ref, dv_ref, out_sem
 ):
-    columns, total, _ = got_ref.shape
+    columns = got_ref.shape[0]
     wide = o_ref.shape[1] // columns
     narrow = dk_ref.shape[1] // columns
 
@@ -102,8 +102,7 @@
             for n, (src, dst, size) in enumerate(pairs)
         ]
 
-    _, slot_col = slot_tables(labels_ref[...], capacity)
-    marks = one_hot_cols(slot_col, total)
+    marks = marks_ref[...]
     for c in range(columns):
         w = slice(c * wide, (c + 1) * wide)
         n = slice(c * narrow, (c + 1) * narrow)
@@ -117,6 +116,11 @@
     for c in range(columns):
         for copy in column(c):
             copy.wait()
+
+
+def home_marks_kernel(capacity, labels_ref, marks_ref):
+    _, slot_col = slot_tables(labels_ref[...], capacity)
+    marks_ref[...] = one_hot_cols(slot_col, marks_ref.shape[1])
 
 
 def attend_kernel(
@@ -216,26 +220,31 @@
 
         return [score, power, finish]
 
-    def product_steps(s):
+    def product_steps(s, heads):
+        part = slice(heads[0] * tok, (heads[-1] + 1) * tok)
+        span = slice(heads[0] * HEAD, (heads[-1] + 1) * HEAD)
         seen = (s + 1) * tok
         rows = block(s)
         turn = s % 2
 
         def rowwise(base, turned, pairs_ref):
             marks = one_hot_rows(slots[s][0], total)
-            result = jnp.dot(turned[:, :seen], pairs_ref[turn, :seen, :], preferred_element_type=F32)
+            result = jnp.dot(turned[:, :seen], pairs_ref[turn, :seen, part], preferred_element_type=F32)
             result = result.astype(BF16)
-            stacked = jnp.concatenate([result[:, h * tok : (h + 1) * tok] for h in range(share)], axis=0)
-            out_ref[s, :, base : base + wide] = lax.dot_general(
+            stacked = jnp.concatenate([result[:, h * tok : (h + 1) * tok] for h in range(len(heads))], axis=0)
+            out_ref[s, :, base + span.start : base + span.stop] = lax.dot_general(
                 marks, stacked, across, preferred_element_type=F32
             ).astype(BF16)
 
         def keywise(total_ref, pairs_ref, base):
-            others = stack(s, base, range(share))
-            result = jnp.dot(pairs_ref[turn, :seen, :], others, preferred_element_type=F32)
+            others = stack(s, base, heads)
+            result = jnp.dot(pairs_ref[turn, :seen, part], others, preferred_element_type=F32)
             if s:
                 total_ref[: s * tok, :] += result[: s * tok]
-            total_ref[rows, :] = result[s * tok :]
+            if heads[0]:
+                total_ref[rows, :] += result[s * tok :]
+            else:
+                total_ref[rows, :] = result[s * tok :]
 
         return [
             lambda: rowwise(0, vt_ref, w_ref),
@@ -244,20 +253,27 @@
             lambda: keywise(dk_ref, ds_ref, 0),
         ]
 
-    receive(0)
-    waiting = []
-    for s in range(columns):
-        lists = [softmax_steps(s, first) for first in range(0, share, joint)]
-        work = [step for group in zip(*lists) for step in group]
-        if s + 1 < columns:
-            waiting = waiting + [lambda n=s + 1: receive(n)]
+    def weave(work, waiting):
         for n, step in enumerate(work):
             step()
             if n < len(waiting):
                 waiting[n]()
         for step in waiting[len(work) :]:
             step()
-        waiting = product_steps(s)
+
+    receive(0)
+    waiting = []
+    for s in range(columns):
+        lists = [softmax_steps(s, first) for first in range(0, share, joint)]
+        if s + 1 < columns:
+            waiting = waiting + [lambda n=s + 1: receive(n)]
+        if s + 1 == columns:
+            for first, work in zip(range(0, share, joint), lists):
+                weave(work, waiting)
+                waiting = product_steps(s, range(first, first + joint))
+        else:
+            weave([step for group in zip(*lists) for step in group], waiting)
+            waiting = product_steps(s, range(share))
     for step in waiting:
         step()
     for s in range(columns):
@@ -292,14 +308,26 @@
     )(labels, queries, grads, keys, values)
 
 
-def unpack(labels, got, wide, capacity):
+def home_marks(labels, total, capacity):
+    near = pl.BlockSpec(memory_space=pltpu.VMEM)
+    return pl.pallas_call(
+        lambda *refs: home_marks_kernel(capacity, *refs),
+        in_specs=[near],
+        out_specs=near,
+        out_shape=jax.ShapeDtypeStruct((labels.shape[1], total), BF16),
+        compiler_params=params(UNPACK_VMEM_BYTES),
+        name="home_marks",
+    )(labels)
+
+
+def unpack(marks, got, wide):
     columns, _, _ = got.shape
-    tok = labels.shape[1]
+    tok = marks.shape[0]
     far = pl.BlockSpec(memory_space=pl.ANY)
     near = pl.BlockSpec(memory_space=pltpu.VMEM)
     shapes = [(tok, columns * size) for size in (wide, wide, HEAD, HEAD)]
     return pl.pallas_call(
-        lambda *refs: unpack_kernel(capacity, *refs),
+        unpack_kernel,
         in_specs=[near, near],
         out_specs=[far] * 4,
         out_shape=[jax.ShapeDtypeStruct(shape, BF16) for shape in shapes],
@@ -309,7 +337,7 @@
         ],
         compiler_params=params(UNPACK_VMEM_BYTES),
         name="unpack_rows",
-    )(labels, got)
+    )(marks, got)
 
 
 def attend(got, sources, starts, capacity):
@@ -364,6 +392,8 @@
         )
     with jax.named_scope("tables"):
         sources = lax.all_gather(source_group, "sp", axis=0, tiled=True)
+        sources, labels = lax.optimization_barrier((sources, dest_group))
+        marks = home_marks(labels, total, capacity)
     with jax.named_scope("to_groups"):
         got = swap(sent, columns, groups)
     with jax.named_scope("attend"):
@@ -371,7 +401,7 @@
     with jax.named_scope("to_homes"):
         back = pltpu.with_memory_space_constraint(swap(done, columns, groups), pltpu.VMEM)
     with jax.named_scope("unpack"):
-        return tuple(unpack(dest_group, back, wide, capacity))
+        return tuple(unpack(marks, back, wide))
 
 
 def solution(mesh):

time: 285 us -> 291 us (1.021)
  blocking collectives: 143 us -> 16.3 us
  waiting for transfers between devices: 103 us -> 222 us
  starting transfers between devices: 15.3 us -> 23.4 us
    all_to_all x1 -> x0, blocking collectives: 127 us -> none  [swap(): lax.all_to_all(blocks, ('sp', 'grp'), split_axis=0, concat_axis=0, tiled=...]
    all_to_all x1 -> x2, waiting for transfers between devices: 103 us -> 222 us  [swap(): lax.all_to_all(blocks, ('sp', 'grp'), split_axis=0, concat_axis=0, tiled=...]
    all_to_all x1 -> x2, starting transfers between devices: 15.3 us -> 23.4 us  [swap(): lax.all_to_all(blocks, ('sp', 'grp'), split_axis=0, concat_axis=0, tiled=...]
  transfers between devices with their start and end apart: 1 -> 2, of which waited for: 1 -> 2; matrix products, arithmetic and copies ran while one was open for 0% -> 0% of each run, Pallas kernels for 0% -> 0%
where the time goes in v6:
time: 291 us; the launch traced here: 289 us
  waiting for transfers between devices  222 us (76%)
  Pallas kernels  24.4 us (8%)
  starting transfers between devices  23.4 us (8%)
  blocking collectives  16.3 us (6%)
    all_to_all x2, waiting for transfers between devices, swap(): lax.all_to_all(blocks, ('sp', 'grp'), split_axis=0, concat_axis=0, tiled=...  222 us
    all_to_all x2, starting transfers between devices, swap(): lax.all_to_all(blocks, ('sp', 'grp'), split_axis=0, concat_axis=0, tiled=...  23.4 us
    all_gather x1, blocking collectives, per_device(): sources = lax.all_gather(source_group, 'sp', axis=0, tiled=True)  16.3 us
    pallas_call x1, Pallas kernels, attend(): pl.pallas_call(lambda *refs: attend_kernel(capacity, *refs), in_specs=[ne...  14.7 us
  transfers between devices with their start and end apart: 2, of which 2 were waited for; matrix products, arithmetic and copies ran while one was open for 0% of the time, Pallas kernels for 0%

profile of v6, /device:TPU:32, one launch (start us, length us, event | category | flops | bytes accessed | tf_op | source)
XLA Modules:
  0.0 289.3 jit_solution(13226441781350821923)
XLA Ops:
  0.6 5.0 %pack_rows.1 = bf16[8,256,1280]{2,1,0:T(8,128)(2,1)} custom-call(s32[1,128]{1,0:T(1,128)} %refs_0_.2, bf16[128,4096]{1,0:T(8,128)(2,1)} %refs_1_.2, bf16[128,4096]{1,0:T(8,128)(2,1)} %refs_2_.1, bf16[128,1024]{1,0:T(8,128)(2,1)} %refs_3_.1, bf16[128,1024]{1,0:T(8,128)(2,1)} %refs_4_.1), custom_call_target="tpu_custom_call" | custom-call | tf_op jit(solution)/shard_map/pack/pack_rows/pallas_call | solution.py:292
  5.6 0.0 copy-start.2
  5.7 15.3 %all-to-all-start = ((bf16[256,8,1280]{2,1,0:T(8,128)(2,1)}), bf16[256,8,1280]{2,1,0:T(8,128)(2,1)}, u32[]{:S(2)}, u32[]{:S(2)}) async-start(bf16[256,8,1280]{2,1,0:T(8,128)(2,1)} %bitcast.7), calls=%async_computation | async-start | bytes 10485760 | tf_op jit(solution)/shard_map/to_groups/all_to_all | solution.py:376
  20.9 0.0 copy-done.2
  20.9 16.3 %all-gather = s32[8,1,128]{2,1,0:T(1,128)} all-gather(s32[1,1,128]{2,1,0:T(1,128)S(1)} %bitcast.9), channel_id=1, replica_groups=mesh['grp'=32,'sp'=8] {'sp'}, dimensions={0}, use_global_device_ids=true | all-gather | bytes 4608 | tf_op jit(solution)/shard_map/tables/all_gather | solution.py:394
  37.2 103.0 %all-to-all-done = bf16[256,8,1280]{2,1,0:T(8,128)(2,1)} async-done(((bf16[256,8,1280]{2,1,0:T(8,128)(2,1)}), bf16[256,8,1280]{2,1,0:T(8,128)(2,1)}, u32[]{:S(2)}, u32[]{:S(2)}) %all-to-all-start) | async-done | bytes 5242912 | tf_op jit(solution)/shard_map/to_groups/all_to_all | solution.py:376
  140.2 14.7 %attend_group.1 = bf16[8,256,1280]{2,1,0:T(8,128)(2,1)S(1)} custom-call(s32[8,128]{1,0:T(8,128)} %bitcast.8, s32[1,1024]{1,0:T(1,128)} %refs_1_.3, bf16[8,256,1280]{2,1,0:T(8,128)(2,1)} %bitcast.3.refs_2_), custom_call_target="tpu_custom_call" | custom-call | tf_op jit(solution)/shard_map/attend/attend_group/pallas_call | solution.py:349
  154.9 0.0 copy-start
  155.0 2.3 copy-done
  157.3 0.0 copy-start.1
  157.3 8.2 %all-to-all-start.1 = ((bf16[256,8,1280]{2,1,0:T(8,128)(2,1)}), bf16[256,8,1280]{2,1,0:T(8,128)(2,1)}, u32[]{:S(2)}, u32[]{:S(2)}) async-start(bf16[256,8,1280]{2,1,0:T(8,128)(2,1)} %bitcast.6), calls=%async_computation.1 | async-start | bytes 10485760 | tf_op jit(solution)/shard_map/to_homes/all_to_all | solution.py:376
  165.4 0.0 copy-done.1
  165.5 0.2 home_marks.1.marks_ref
  165.7 119.0 %all-to-all-done.1 = bf16[256,8,1280]{2,1,0:T(8,128)(2,1)} async-done(((bf16[256,8,1280]{2,1,0:T(8,128)(2,1)}), bf16[256,8,1280]{2,1,0:T(8,128)(2,1)}, u32[]{:S(2)}, u32[]{:S(2)}) %all-to-all-start.1) | async-done | bytes 5242912 | tf_op jit(solution)/shard_map/to_homes/all_to_all | solution.py:376
  284.7 4.4 %unpack_rows.1 = (bf16[128,4096]{1,0:T(8,128)(2,1)}, bf16[128,4096]{1,0:T(8,128)(2,1)}, bf16[128,1024]{1,0:T(8,128)(2,1)}, bf16[128,1024]{1,0:T(8,128)(2,1)}) custom-call(bf16[128,256]{1,0:T(8,128)(2,1)S(1)} %home_marks.1.marks_ref, bf16[8,256,1280]{2,1,0:T(8,128)(2,1)} %bitcast.5.got_ref), custom_call_target="tpu_custom_call" | custom-call | tf_op jit(solution)/shard_map/unpack/unpack_rows/pallas_call | solution.py:329
Async XLA Ops:
  5.6 15.3 %copy-start.2 = (s32[1,128]{1,0:T(1,128)S(1)}, s32[1,128]{1,0:T(1,128)}, u32[]{:S(2)}) copy-start(s32[1,128]{1,0:T(1,128)} %param.12) | copy-start | bytes 1540
  5.7 134.6 %all-to-all-start = ((bf16[256,8,1280]{2,1,0:T(8,128)(2,1)}), bf16[256,8,1280]{2,1,0:T(8,128)(2,1)}, u32[]{:S(2)}, u32[]{:S(2)}) async-start(bf16[256,8,1280]{2,1,0:T(8,128)(2,1)} %bitcast.7), calls=%async_computation | async-start | bytes 10485760 | tf_op jit(solution)/shard_map/to_groups/all_to_all | solution.py:376
  154.9 2.3 copy-start
  157.3 8.2 %copy-start.1 = (s32[1,128]{1,0:T(1,128)S(1)}, s32[1,128]{1,0:T(1,128)}, u32[]{:S(2)}) copy-start(s32[1,128]{1,0:T(1,128)} %refs_0_.2) | copy-start | bytes 1540
  157.3 127.4 %all-to-all-start.1 = ((bf16[256,8,1280]{2,1,0:T(8,128)(2,1)}), bf16[256,8,1280]{2,1,0:T(8,128)(2,1)}, u32[]{:S(2)}, u32[]{:S(2)}) async-start(bf16[256,8,1280]{2,1,0:T(8,128)(2,1)} %bitcast.6), calls=%async_computation.1 | async-start | bytes 10485760 | tf_op jit(solution)/shard_map/to_homes/all_to_all | solution.py:376
